TPU v7x, 256 devices: a whole 4x4x8 slice. The times are simulated.
256 devices in a mesh: dp: 4 (over y_hi, core), tm: 8 (over x, y_lo), mp: 8 (over z).
Axes of the slice: x: 4, y: 4 (y_hi: 2, y_lo: 2; y = y_hi * 2 + y_lo), z: 8, core: 2. Of those that a mesh axis runs over, the one named last changes fastest.
Arguments:
- spans: bfloat16 [4, 16, 256, 4096], P('dp', 'tm', None, 'mp'), may hold values from -6 to 6
- frame_span: int32 [4, 8], P('dp', 'tm'), may hold values from 0 to 1
- norm_gain: bfloat16 [4096], P('mp'), may hold values from 0.5 to 6
- w_query: bfloat16 [4096, 2048], P(('dp', 'tm'), 'mp'), may hold values from -0.09375 to 0.09375
- w_key: bfloat16 [4096, 2048], P(('dp', 'tm'), 'mp'), may hold values from -0.09375 to 0.09375
- w_value: bfloat16 [4096, 2048], P(('dp', 'tm'), 'mp'), may hold values from -0.09375 to 0.09375
- w_out: bfloat16 [2048, 4096], P('mp', ('dp', 'tm')), may hold values from -0.125 to 0.125
- grad_out: bfloat16 [4, 8, 256, 4096], P('dp', 'tm', None, 'mp'), may hold values from -6 to 6
Outputs:
- span_grad: bfloat16 [4, 16, 256, 4096], P('dp', 'tm', None, 'mp')
- grad_w_query: float32 [4096, 2048], P(('dp', 'tm'), 'mp')
- grad_w_key: float32 [4096, 2048], P(('dp', 'tm'), 'mp')
- grad_w_value: float32 [4096, 2048], P(('dp', 'tm'), 'mp')
- grad_w_out: float32 [2048, 4096], P('mp', ('dp', 'tm'))
Inputs may be any that keep to these rules, and one draw needn't show every extreme that they name: Frame f of clip c reads stored span (f) * 2 + frame_span[c, f] of the same clip; each span is read by at most one frame, and a span that no frame reads gets zero gradient.
All inputs are finite; a program needn't handle non-finite values.
Results may differ from a plain program's by a relative error of at most 0.03.
The roundings to bfloat16 on the way count: a program that leaves them out, or rounds other values in their place, can miss the bound.
Values may be sent and summed in bfloat16 or wider, within the bound.
A program may use at most 128 MiB of HBM per device.

v0:
```python
import jax
import jax.numpy as jnp
from jax import lax
from jax.sharding import PartitionSpec as P

HS = 128


EPSILON = 1e-05


def attend(pieces):
    queries, key_rows, value_rows, att_grad = pieces
    clips, frames_all, patches, width = queries.shape
    heads = width // HS

    def split_heads(array):
        return array.reshape(clips, frames_all, patches, heads, HS)

    def join_heads(array):
        return array.reshape(clips, frames_all, patches, width)

    query_h = split_heads(queries)
    key_h = split_heads(key_rows)
    value_h = split_heads(value_rows)
    grad_h = split_heads(att_grad)
    scale = HS ** (-0.5)
    scores = (
        jnp.einsum("cfphd,cgphd->cphfg", query_h, key_h, preferred_element_type=jnp.float32) * scale
    )
    causal = jnp.arange(frames_all)[:, None] >= jnp.arange(frames_all)[None, :]
    scores = jnp.where(causal, scores, -1e30)
    peak = jnp.max(scores, axis=-1, keepdims=True)
    expo = jnp.exp(scores - peak)
    soft = expo / jnp.sum(expo, axis=-1, keepdims=True)
    soft_b = soft.astype(jnp.bfloat16)
    att_out = jnp.einsum(
        "cphfg,cgphd->cfphd", soft_b, value_h, preferred_element_type=jnp.float32
    ).astype(jnp.bfloat16)
    dsoft = jnp.einsum("cfphd,cgphd->cphfg", grad_h, value_h, preferred_element_type=jnp.float32)
    dscore = (soft * (dsoft - jnp.sum(dsoft * soft, axis=-1, keepdims=True)) * scale).astype(
        jnp.bfloat16
    )
    grad_query = jnp.einsum(
        "cphfg,cgphd->cfphd", dscore, key_h, preferred_element_type=jnp.float32
    ).astype(jnp.bfloat16)
    grad_key = jnp.einsum(
        "cphfg,cfphd->cgphd", dscore, query_h, preferred_element_type=jnp.float32
    ).astype(jnp.bfloat16)
    grad_value = jnp.einsum(
        "cphfg,cfphd->cgphd", soft_b, grad_h, preferred_element_type=jnp.float32
    ).astype(jnp.bfloat16)
    return (
        join_heads(att_out),
        join_heads(grad_query),
        join_heads(grad_key),
        join_heads(grad_value),
    )


def attend_items(pieces):
    clips, frames_all, single, items, width = pieces[0].shape
    flat = tuple((piece.reshape(clips, frames_all, items, width) for piece in pieces))
    results = attend(flat)
    return tuple((result.reshape(clips, frames_all, single, items, width) for result in results))


def local(spans, frame_span, norm_gain, w_query, w_key, w_value, w_out, grad_out):
    stored = spans.shape[1]
    frames_dev = grad_out.shape[1]
    patches = grad_out.shape[2]
    head_cols = w_query.shape[1]
    tokens = frames_dev * patches
    contract_rows = (((0,), (0,)), ((), ()))
    contract_cols = (((1,), (1,)), ((), ()))
    picker = frame_span[0][:, None] == jnp.arange(stored, dtype=jnp.int32)[None, :]
    picker_f = picker.astype(jnp.float32)
    frames = jnp.einsum(
        "fs,bspd->bfpd", picker.astype(jnp.bfloat16), spans, preferred_element_type=jnp.float32
    ).astype(jnp.bfloat16)
    full_x, full_dy, full_gain = (
        lax.all_gather(frames, "mp", axis=3, tiled=True),
        lax.all_gather(grad_out, "mp", axis=3, tiled=True),
        lax.all_gather(norm_gain, "mp", axis=0, tiled=True),
    )
    width = full_x.shape[3]
    x_flat = full_x.reshape(tokens, width).astype(jnp.float32)
    gain_all = full_gain.astype(jnp.float32)
    inverse = lax.rsqrt(jnp.mean(x_flat * x_flat, axis=1, keepdims=True) + EPSILON)
    normed = (x_flat * inverse * gain_all).astype(jnp.bfloat16)
    dy_flat = full_dy.reshape(tokens, width)
    pieces = (
        lax.all_gather(w_query, ("dp", "tm"), axis=0, tiled=True),
        lax.all_gather(w_key, ("dp", "tm"), axis=0, tiled=True),
        lax.all_gather(w_value, ("dp", "tm"), axis=0, tiled=True),
    )
    columns = normed
    sums_query, sums_key, sums_value = tuple(
        (
            jnp.dot(columns, weight_piece, preferred_element_type=jnp.float32)
            for weight_piece in pieces
        )
    )
    columns = dy_flat
    sums_out = lax.dot_general(
        columns,
        lax.all_gather(w_out, ("dp", "tm"), axis=1, tiled=True),
        contract_cols,
        preferred_element_type=jnp.float32,
    )
    queries = sums_query.astype(jnp.bfloat16)
    key_rows = sums_key.astype(jnp.bfloat16)
    value_rows = sums_value.astype(jnp.bfloat16)
    att_grad = sums_out.astype(jnp.bfloat16)
    groups = lax.axis_size("tm")
    shape5 = (1, frames_dev, groups, patches // groups, head_cols)
    patch_att, patch_gq, patch_gk, patch_gv = attend_items(
        (
            lax.all_to_all(queries.reshape(shape5), "tm", split_axis=2, concat_axis=1, tiled=True),
            lax.all_to_all(key_rows.reshape(shape5), "tm", split_axis=2, concat_axis=1, tiled=True),
            lax.all_to_all(
                value_rows.reshape(shape5), "tm", split_axis=2, concat_axis=1, tiled=True
            ),
            lax.all_to_all(att_grad.reshape(shape5), "tm", split_axis=2, concat_axis=1, tiled=True),
        )
    )
    frame_att, frame_gq, frame_gk, frame_gv = (
        lax.all_to_all(patch_att, "tm", split_axis=1, concat_axis=2, tiled=True),
        lax.all_to_all(patch_gq, "tm", split_axis=1, concat_axis=2, tiled=True),
        lax.all_to_all(patch_gk, "tm", split_axis=1, concat_axis=2, tiled=True),
        lax.all_to_all(patch_gv, "tm", split_axis=1, concat_axis=2, tiled=True),
    )
    att_out = frame_att.reshape(tokens, head_cols)
    grad_query = frame_gq.reshape(tokens, head_cols)
    grad_key = frame_gk.reshape(tokens, head_cols)
    grad_value = frame_gv.reshape(tokens, head_cols)
    pieces = lax.all_gather((w_query, w_key, w_value), ("dp", "tm"), axis=0, tiled=True)
    result = lax.dot_general(
        grad_query, pieces[0], contract_cols, preferred_element_type=jnp.float32
    )
    result = result + lax.dot_general(
        grad_key, pieces[1], contract_cols, preferred_element_type=jnp.float32
    )
    grad_normed = result + lax.dot_general(
        grad_value, pieces[2], contract_cols, preferred_element_type=jnp.float32
    )
    scaled = grad_normed * gain_all
    inner = jnp.mean(scaled * x_flat, axis=1, keepdims=True)
    branch_full = inverse * scaled - x_flat * inverse**3 * inner
    branch = lax.psum_scatter(
        branch_full.reshape(1, frames_dev, patches, width).astype(jnp.bfloat16),
        "mp",
        scatter_dimension=3,
        tiled=True,
    ).astype(jnp.float32)
    grad_frames = grad_out.astype(jnp.float32) + branch
    span_grad = jnp.einsum(
        "fs,bfpd->bspd", picker_f, grad_frames, precision=lax.Precision.HIGHEST
    ).astype(jnp.bfloat16)
    grads_cat = jnp.concatenate([grad_query, grad_key, grad_value], axis=1)
    columns = normed
    projected = lax.dot_general(
        columns, grads_cat, contract_rows, preferred_element_type=jnp.float32
    )
    outer = lax.dot_general(dy_flat, att_out, contract_rows, preferred_element_type=jnp.float32)
    summed = lax.psum_scatter(
        jnp.concatenate([projected, outer], axis=1).astype(jnp.bfloat16),
        ("dp", "tm"),
        scatter_dimension=0,
        tiled=True,
    ).astype(jnp.float32)
    return (
        span_grad,
        summed[:, :head_cols],
        summed[:, head_cols : 2 * head_cols],
        summed[:, 2 * head_cols : 3 * head_cols],
        summed[:, 3 * head_cols :].T,
    )


def solution(mesh):
    placed = (
        P("dp", "tm", None, "mp"),
        P("dp", "tm"),
        P("mp"),
        P(("dp", "tm"), "mp"),
        P(("dp", "tm"), "mp"),
        P(("dp", "tm"), "mp"),
        P("mp", ("dp", "tm")),
        P("dp", "tm", None, "mp"),
    )
    return jax.shard_map(
        local,
        mesh=mesh,
        in_specs=placed,
        out_specs=(
            P("dp", "tm", None, "mp"),
            P(("dp", "tm"), "mp"),
            P(("dp", "tm"), "mp"),
            P(("dp", "tm"), "mp"),
            P("mp", ("dp", "tm")),
        ),
        check_vma=False,
    )
```

profile of v0, /device:TPU:1, one launch (start us, length us, event | category | flops | bytes accessed | tf_op | source)
XLA Modules:
  0.0 735.1 jit_solution(12638865905517727789)
XLA Ops:
  8.9 0.7 copy.93
  13.6 21.7 %all-gather.1 = bf16[8,1,512]{2,1,0:T(2,128)(2,1)S(1)} all-gather(bf16[1,1,512]{2,1,0:T(2,128)(2,1)S(1)} %reshape.216), channel_id=1, replica_groups=mesh['dp'=4,'tm'=8,'mp'=8] {'mp'}, dimensions={0}, use_global_device_ids=true | all-gather | bytes 9216 | tf_op jit(solution)/shard_map/all_gather | solution.py:84
  35.8 15.9 %all-gather.19.cloned.1.call-done = bf16[256,4096]{1,0:T(8,128)(2,1)} async-done(((bf16[256,512]{1,0:T(8,128)(2,1)}), bf16[256,4096]{1,0:T(8,128)(2,1)}) %all-gather.19.cloned.1.call-update) | async-done | bytes 2097168 | tf_op jit(solution)/shard_map/all_gather | solution.py:82
  51.8 2.2 fusion.5
  54.6 38.7 %all-gather.13.cloned.1.call-done = bf16[1,1,256,4096]{3,2,1,0:T(8,128)(2,1)} async-done(((bf16[1,1,256,512]{3,2,1,0:T(8,128)(2,1)}), bf16[1,1,256,4096]{3,2,1,0:T(8,128)(2,1)}) %all-gather.13.cloned.1.call-update) | async-done | bytes 2097168 | tf_op jit(solution)/shard_map/all_gather | solution.py:83
  93.3 82.7 %all-gather.15.cloned.1.call-done = bf16[256,4096]{1,0:T(8,128)(2,1)} async-done(((bf16[256,128]{1,0:T(8,128)(2,1)}), bf16[256,4096]{1,0:T(8,128)(2,1)}) %all-gather.15.cloned.1.call-update) | async-done | bytes 2097168 | tf_op jit(solution)/shard_map/all_gather | solution.py:107
  176.0 3.6 fusion.22
  179.6 3.8 all-to-all-start.2
  183.4 78.5 %all-gather.17.cloned.1.call-done = bf16[4096,256]{1,0:T(8,128)(2,1)} async-done(((bf16[128,256]{1,0:T(8,128)(2,1)}), bf16[4096,256]{1,0:T(8,128)(2,1)}) %all-gather.17.cloned.1.call-update) | async-done | bytes 2097168 | tf_op jit(solution)/shard_map/all_gather | solution.py:95
  261.9 3.0 convolution_convert_fusion.6
  264.9 5.0 all-to-all-start.3
  269.9 79.2 %all-gather.11.cloned.1.call-done = bf16[4096,256]{1,0:T(8,128)(2,1)} async-done(((bf16[128,256]{1,0:T(8,128)(2,1)}), bf16[4096,256]{1,0:T(8,128)(2,1)}) %all-gather.11.cloned.1.call-update) | async-done | bytes 2097168 | tf_op jit(solution)/shard_map/all_gather | solution.py:93
  349.1 3.0 convolution_convert_fusion.7
  352.1 5.0 all-to-all-start.1
  357.1 79.1 %all-gather.9.cloned.1.call-done = bf16[4096,256]{1,0:T(8,128)(2,1)} async-done(((bf16[128,256]{1,0:T(8,128)(2,1)}), bf16[4096,256]{1,0:T(8,128)(2,1)}) %all-gather.9.cloned.1.call-update) | async-done | bytes 2097168 | tf_op jit(solution)/shard_map/all_gather | solution.py:94
  436.2 3.0 convolution_convert_fusion.8
  439.3 5.0 all-to-all-start
  444.6 5.0 all-to-all-done
  449.7 1.7 fusion.72
  452.0 1.2 fusion.27
  453.3 0.7 reshape_reshape.18
  454.1 1.4 fusion.25
  455.6 0.7 reshape_reshape.16
  456.4 3.4 all-to-all-start.4
  459.7 1.4 fusion.26
  461.3 0.7 reshape_reshape.17
  462.0 2.9 all-to-all-done.4
  464.9 3.4 all-to-all-start.5
  468.3 4.3 fusion.77
  472.6 0.9 all-to-all-done.5
  473.5 4.2 all-to-all-start.6
  477.7 5.5 convolution_add_fusion.1
  483.3 3.9 fusion.4
  487.1 2.8 fusion.11
  490.2 1.2 fusion.28
  491.6 10.2 %all_to_all.32 = bf16[1,8,1,32,256]{4,3,2,0,1:T(8,128)(2,1)S(1)} all-to-all(bf16[1,8,1,32,256]{4,3,2,0,1:T(8,128)(2,1)S(1)} %bitcast.106), channel_id=1, replica_groups=mesh['dp'=4,'tm'=8,'mp'=8] {'tm'}, dimensions={1} | all-to-all | bytes 262144 | tf_op jit(solution)/shard_map/all_to_all | solution.py:128
  501.8 3.7 fusion.3
  505.5 4.6 convolution_convert_fusion
  510.1 7.8 %pad_maximum_fusion = bf16[4096,1024]{0,1:T(8,128)(2,1)} fusion(bf16[4096,256]{0,1:T(8,128)(2,1)} %fusion.3, bf16[4096,768]{0,1:T(8,128)(2,1)} %convolution_convert_fusion), kind=kLoop, calls=%fused_computation.2 | loop fusion | flops 16777216 | bytes 16777216 | tf_op jit(solution)/shard_map/concatenate | solution.py:167
  517.9 12.0 %copy.64 = bf16[4096,1024]{1,0:T(8,128)(2,1)} copy(bf16[4096,1024]{0,1:T(8,128)(2,1)} %pad_maximum_fusion) | data formatting | bytes 16777216
  530.0 2.2 reduce-scatter.5.cloned.1.call-done
  532.2 1.0 add_bitcast_fusion
  533.2 0.9 fusion.29
  534.2 189.9 %reduce-scatter.7.cloned.1.call-done = bf16[128,1024]{1,0:T(8,128)(2,1)} async-done(((bf16[4096,1024]{1,0:T(8,128)(2,1)}), bf16[128,1024]{1,0:T(8,128)(2,1)}) %reduce-scatter.7.cloned.1.call-update) | async-done | bytes 262160
  724.1 1.1 copy.65
  725.3 0.8 copy.59
  726.1 0.8 copy.58
  726.8 0.8 copy.57
  (58 shorter events, 8.7 us)
Async XLA Ops:
  7.2 1.1 copy-start
  7.2 44.6 %all-gather.19.cloned.1.call-start = ((), (), s32[]{:S(2)}) async-start(), calls=%async_computation.16 | async-start | bytes 2359296 | tf_op jit(solution)/shard_map/all_gather | solution.py:82
  9.7 83.6 %all-gather.13.cloned.1.call-start = ((), (), s32[]{:S(2)}) async-start(), calls=%async_computation.12 | async-start | bytes 2359296 | tf_op jit(solution)/shard_map/all_gather | solution.py:83
  10.4 165.5 %all-gather.15.cloned.1.call-start = ((), (), s32[]{:S(2)}) async-start(), calls=%async_computation.13 | async-start | bytes 2162688 | tf_op jit(solution)/shard_map/all_gather | solution.py:107
  11.2 250.8 %all-gather.17.cloned.1.call-start = ((), (), s32[]{:S(2)}) async-start(), calls=%async_computation.14 | async-start | bytes 2162688 | tf_op jit(solution)/shard_map/all_gather | solution.py:95
  11.7 337.3 %all-gather.11.cloned.1.call-start = ((), (), s32[]{:S(2)}) async-start(), calls=%async_computation.11 | async-start | bytes 2162688 | tf_op jit(solution)/shard_map/all_gather | solution.py:93
  12.3 423.9 %all-gather.9.cloned.1.call-start = ((), (), s32[]{:S(2)}) async-start(), calls=%async_computation.10 | async-start | bytes 2162688 | tf_op jit(solution)/shard_map/all_gather | solution.py:94
  51.8 210.1 %copy-start.1 = (bf16[256,4096]{1,0:T(8,128)(2,1)S(1)}, bf16[256,4096]{1,0:T(8,128)(2,1)}, u32[]{:S(2)}) copy-start(bf16[256,4096]{1,0:T(8,128)(2,1)} %all-gather.19.cloned.1.call-done) | copy-start | bytes 6291460
  54.6 381.6 %copy-start.4 = (f32[256]{0:T(256)}, f32[256]{0:T(256)S(1)}, u32[]{:S(2)}) copy-start(f32[256]{0:T(256)S(1)} %get-tuple-element.24) | copy-start | bytes 3076
  179.6 85.3 %all-to-all-start.2 = ((bf16[1,1,8,32,256]{4,3,1,0,2:T(8,128)(2,1)}), bf16[1,1,8,32,256]{4,3,1,0,2:T(8,128)(2,1)S(1)}, u32[]{:S(2)}, u32[]{:S(2)}) async-start(bf16[1,1,8,32,256]{4,3,1,0,2:T(8,128)(2,1)} %bitcast.12), calls=%async_computation.2 | async-start | bytes 262144 | tf_op jit(solution)/shard_map/all_to_all | solution.py:124
  264.9 87.1 %all-to-all-start.3 = ((bf16[1,1,8,32,256]{4,3,1,0,2:T(8,128)(2,1)}), bf16[1,1,8,32,256]{4,3,1,0,2:T(8,128)(2,1)S(1)}, u32[]{:S(2)}, u32[]{:S(2)}) async-start(bf16[1,1,8,32,256]{4,3,1,0,2:T(8,128)(2,1)} %bitcast.14), calls=%async_computation.3 | async-start | bytes 262144 | tf_op jit(solution)/shard_map/all_to_all | solution.py:121
  352.1 87.2 %all-to-all-start.1 = ((bf16[1,1,8,32,256]{4,3,1,0,2:T(8,128)(2,1)}), bf16[1,1,8,32,256]{4,3,1,0,2:T(8,128)(2,1)S(1)}, u32[]{:S(2)}, u32[]{:S(2)}) async-start(bf16[1,1,8,32,256]{4,3,1,0,2:T(8,128)(2,1)} %bitcast.9), calls=%async_computation.1 | async-start | bytes 262144 | tf_op jit(solution)/shard_map/all_to_all | solution.py:119
  439.3 10.3 %all-to-all-start = ((bf16[1,1,8,32,256]{4,3,1,0,2:T(8,128)(2,1)}), bf16[1,1,8,32,256]{4,3,1,0,2:T(8,128)(2,1)S(1)}, u32[]{:S(2)}, u32[]{:S(2)}) async-start(bf16[1,1,8,32,256]{4,3,1,0,2:T(8,128)(2,1)} %bitcast.7), calls=%async_computation | async-start | bytes 262144 | tf_op jit(solution)/shard_map/all_to_all | solution.py:120
  444.6 11.7 %copy-start.3 = (bf16[8,32,2,128]{3,2,1,0:T(2,128)(2,1)}, bf16[8,32,2,128]{3,2,1,0:T(2,128)(2,1)S(1)}, u32[]{:S(2)}) copy-start(bf16[8,32,2,128]{3,2,1,0:T(2,128)(2,1)S(1)} %reshape.201) | copy-start | bytes 393220
  451.4 0.6 copy-start.7
  456.4 8.6 %all-to-all-start.4 = ((bf16[1,8,1,32,256]{4,3,2,0,1:T(8,128)(2,1)}), bf16[1,8,1,32,256]{4,3,2,0,1:T(8,128)(2,1)S(1)}, u32[]{:S(2)}, u32[]{:S(2)}) async-start(bf16[1,8,1,32,256]{4,3,2,0,1:T(8,128)(2,1)} %bitcast.17), calls=%async_computation.4 | async-start | bytes 262144 | tf_op jit(solution)/shard_map/all_to_all | solution.py:129
  464.9 8.6 %all-to-all-start.5 = ((bf16[1,8,1,32,256]{4,3,2,0,1:T(8,128)(2,1)}), bf16[1,8,1,32,256]{4,3,2,0,1:T(8,128)(2,1)S(1)}, u32[]{:S(2)}, u32[]{:S(2)}) async-start(bf16[1,8,1,32,256]{4,3,2,0,1:T(8,128)(2,1)} %bitcast.21), calls=%async_computation.5 | async-start | bytes 262144 | tf_op jit(solution)/shard_map/all_to_all | solution.py:130
  473.5 9.7 %all-to-all-start.6 = ((bf16[1,8,1,32,256]{4,3,2,0,1:T(8,128)(2,1)}), bf16[1,8,1,32,256]{4,3,2,0,1:T(8,128)(2,1)S(1)}, u32[]{:S(2)}, u32[]{:S(2)}) async-start(bf16[1,8,1,32,256]{4,3,2,0,1:T(8,128)(2,1)} %bitcast.25), calls=%async_computation.6 | async-start | bytes 262144 | tf_op jit(solution)/shard_map/all_to_all | solution.py:131
  477.7 54.5 %reduce-scatter.5.cloned.1.call-start = ((), (), s32[]{:S(2)}) async-start(), calls=%async_computation.15 | async-start | bytes 2359296 | tf_op jit(solution)/shard_map/reduce_scatter | solution.py:150
  483.2 3.9 copy-start.5
  483.2 3.9 copy-start.6
  487.1 3.0 copy-start.8
  489.9 234.2 %reduce-scatter.7.cloned.1.call-start = ((), (), s32[]{:S(2)}) async-start(), calls=%async_computation.17 | async-start | bytes 8650752
  529.9 2.3 copy-start.2
Sparse Core Ops, SparseCore 0:
  10.4 41.3 all-gather.18
  53.6 39.6 all-gather.12
  95.0 80.8 all-gather.14
  177.6 84.2 all-gather.16
  263.6 85.4 all-gather.10
  350.7 85.4 all-gather.8
  490.1 42.1 reduce-scatter.4
  534.8 189.3 reduce-scatter.6
where the time goes:
time: 739 us; the launch traced here: 735 us
  waiting for transfers between devices  578 us (78%)
  matrix products  42.5 us (6%)
  blocking collectives  31.8 us (4%)
  starting transfers between devices  30.2 us (4%)
  local copies, waits for them, and re-layouts  21.4 us (3%)
  other arithmetic  16 us (2%)
  between operations  15.1 us (2%)
    unnamed x9, waiting for transfers between devices  193 us
    all_gather x1, waiting for transfers between devices, local(): lax.all_gather(w_out, ('dp', 'tm'), axis=1, tiled=True)  82.7 us
    all_gather x1, waiting for transfers between devices, local(): lax.all_gather(w_query, ('dp', 'tm'), axis=0, tiled=True)  79.2 us
    all_gather x1, waiting for transfers between devices, local(): lax.all_gather(w_key, ('dp', 'tm'), axis=0, tiled=True)  79.1 us
    all_gather x1, waiting for transfers between devices, local(): lax.all_gather(w_value, ('dp', 'tm'), axis=0, tiled=True)  78.5 us
    all_gather x1, waiting for transfers between devices, local(): lax.all_gather(grad_out, 'mp', axis=3, tiled=True)  38.7 us
    all_gather x1, blocking collectives, local(): lax.all_gather(norm_gain, 'mp', axis=0, tiled=True)  21.7 us
    unnamed x24, local copies, waits for them, and re-layouts  17.1 us
  transfers between devices with their start and end apart: 15, of which 11 were waited for; matrix products, arithmetic and copies ran while one was open for 8% of the time, Pallas kernels for 0%

commit v1 on v0

v1 whole, which is shorter than its diff:
```python
import jax
import jax.numpy as jnp
from jax import lax
from jax.experimental import pallas as pl
from jax.experimental.pallas import tpu as pltpu
from jax.sharding import PartitionSpec as P

HS = 128
EPSILON = 1e-05
BF = jnp.bfloat16
F32 = jnp.float32
MESH = pl.DeviceIdType.MESH
COPIES = 160

ROWS_COLS = (((1,), (1,)), ((), ()))


def dot(left, right):
    return jnp.dot(left, right, preferred_element_type=F32)


def dot_t(left, right):
    return lax.dot_general(left, right, ROWS_COLS, preferred_element_type=F32)


class Copies:
    def __init__(self, send, recv):
        self.send = send
        self.recv = recv
        self.started = []

    def __call__(self, src, dst, device):
        at = len(self.started)
        assert at < COPIES
        copy = pltpu.make_async_remote_copy(
            src_ref=src,
            dst_ref=dst,
            send_sem=self.send.at[at],
            recv_sem=self.recv.at[at],
            device_id=device,
            device_id_type=MESH,
        )
        copy.start()
        self.started.append(copy)
        return copy


def kernel(
    x_ref,
    dy_ref,
    gain_ref,
    wq_ref,
    wk_ref,
    wv_ref,
    wo_ref,
    gf_ref,
    gq_ref,
    gk_ref,
    gv_ref,
    go_ref,
    xn,
    dy,
    wp,
    wg,
    ss,
    sl,
    iv,
    aq,
    aa,
    sb,
    rb,
    ob,
    gb,
    gc,
    gt,
    ts,
    tr,
    tl,
    tt,
    ps,
    sr,
    po,
    cs,
    cr,
    wt,
    ra,
    ta,
    r1,
    rc,
    tc,
    rf,
    fs,
    fr,
    fh,
    send,
    recv,
):
    dp = lax.axis_index("dp")
    tm = lax.axis_index("tm")
    mp = lax.axis_index("mp")
    core = lax.rem(dp, 2)
    other = 1 - core
    yh = lax.div(dp, 2)
    x = lax.div(tm, 2)
    yl = lax.rem(tm, 2)
    y = yh * 2 + yl

    def device(x_at, y_at):
        return (lax.div(y_at, 2) * 2 + core, x_at * 2 + lax.rem(y_at, 2), mp)

    def ring8(offset):
        return lax.rem(mp + offset + 8, 8)

    def along_z(offset):
        return (dp, tm, ring8(offset))

    def along_tm(offset):
        return (dp, lax.rem(tm + offset, 8), mp)

    sibling = (yh * 2 + other, tm, mp)
    zr, zl = along_z(1), along_z(-1)
    x1, x2, x3 = (lax.rem(x + k, 4) for k in (1, 2, 3))
    y1, y2, y3 = (lax.rem(y + k, 4) for k in (1, 2, 3))
    xr, xl = device(x1, y), device(x3, y)
    yr, yd = device(x, y1), device(x, y3)
    far_y = device(x, lax.rem(y + 3 + 2 * yl, 4))

    def hi(v):
        return lax.div(v, 2)

    def lo(v):
        return lax.rem(v, 2)

    barrier = pltpu.get_barrier_semaphore()
    partners = [sibling, far_y]
    partners += [along_z(k) for k in range(1, 8)]
    partners += [along_tm(k) for k in range(1, 8)]
    for partner in partners:
        pl.semaphore_signal(barrier, inc=1, device_id=partner, device_id_type=MESH)
    pl.semaphore_wait(barrier, len(partners))

    copy = Copies(send, recv)

    class Ring:
        def __init__(self, src, ref):
            self.ref = ref
            home = ref.at[mp, core]
            self.right = copy(src, home, zr)
            self.left = copy(src, home, zl)
            self.pending = [copy(src, home, sibling)]
            self.step = 1

        def advance(self):
            k = self.step
            self.step += 1
            ref = self.ref
            self.right.wait_recv()
            if k < 4:
                block = ref.at[ring8(-k), core]
                part = block if k < 3 else block.at[pl.ds(0, 128)]
                self.right = copy(part, part, zr)
                self.pending.append(copy(block, block, sibling))
            self.left.wait_recv()
            if k < 4:
                block = ref.at[ring8(k), core]
                part = block if k < 3 else block.at[pl.ds(128, 128)]
                self.left = copy(part, part, zl)
                self.pending.append(copy(block, block, sibling))
            else:
                block = ref.at[ring8(4), core]
                self.pending.append(copy(block, block, sibling))

        def settle(self):
            for c in self.pending:
                c.wait_recv()
            self.pending = []

    ring_dy = Ring(dy_ref, dy)

    for h in range(2):
        for a, ref in enumerate((wq_ref, wk_ref, wv_ref)):
            wp[h, :, a * HS : (a + 1) * HS] = ref[:, h * HS : (h + 1) * HS]
        wp[h, :, 3 * HS :] = wo_ref[h * HS : (h + 1) * HS, :].astype(F32).T.astype(BF)
    xh, xlo = hi(x), lo(x)
    mine = wg.at[yh, core, xh, xlo, yl]
    pair = copy(wp.at[other], mine, sibling)

    sums = jnp.zeros((256, HS), F32)
    for g in range(4):
        part = x_ref[:, g * HS : (g + 1) * HS].astype(F32)
        sums = sums + part * part
    row = jnp.sum(sums.T, axis=0, keepdims=True)
    sl[...] = jnp.broadcast_to(row, (8, 256))
    sumsq = [copy(sl, ss.at[mp], along_z(k)) for k in range(1, 8)]
    ss[mp] = sl[...]
    wg[yh, core, xh, xlo, yl] = wp[core]
    dy[mp, core] = dy_ref[...]

    pair.wait_recv()

    def block(x_at, y_at, s):
        return wg.at[hi(y_at), s, hi(x_at), lo(x_at), lo(y_at)]

    def upper(ref):
        return ref.at[pl.ds(0, 64)]

    def lower(ref):
        return ref.at[pl.ds(64, 64)]

    own_a, own_b = block(x, y, 0), block(x, y, 1)
    a_r, a_l = copy(own_a, own_a, xr), copy(own_a, own_a, xl)
    b_r, b_l = copy(own_b, own_b, yr), copy(own_b, own_b, yd)

    for c in sumsq:
        c.wait_recv()
    total = ss[0]
    for k in range(1, 8):
        total = total + ss[k]
    inv_row = lax.rsqrt(total / 4096.0 + EPSILON)
    iv[...] = jnp.broadcast_to(inv_row[0:1, :], (HS, 256)).T
    for g in range(4):
        cols = slice(g * HS, (g + 1) * HS)
        xn[mp, core, :, cols] = (
            x_ref[:, cols].astype(F32) * iv[...] * gain_ref[:, cols].astype(F32)
        ).astype(BF)
    ring_xn = Ring(xn.at[mp, core], xn)

    a_r.wait_recv()
    near = upper(block(x3, y, 0))
    a_r = copy(near, near, xr)
    a_l.wait_recv()
    near = lower(block(x1, y, 0))
    a_l = copy(near, near, xl)
    b_r.wait_recv()
    near = upper(block(x, y3, 1))
    b_r = copy(near, near, yr)
    b_l.wait_recv()
    near = lower(block(x, y1, 1))
    b_l = copy(near, near, yd)

    aq[...] = jnp.zeros_like(aq)
    aa[...] = jnp.zeros_like(aa)

    ring_dy.advance()

    for c in (a_r, a_l, b_r, b_l):
        c.wait_recv()

    def row_a(y_at):
        return wg.at[hi(y_at), 0, :, :, lo(y_at)]

    def row_b(x_at):
        return wg.at[:, 1, hi(x_at), lo(x_at), :]

    a_r, a_l = copy(row_a(y), row_a(y), yr), copy(row_a(y), row_a(y), yd)
    b_r, b_l = copy(row_b(x), row_b(x), xr), copy(row_b(x), row_b(x), xl)

    ring_xn.advance()
    ring_dy.advance()

    a_r.wait_recv()
    near = row_a(y3).at[0]
    a_r = copy(near, near, yr)
    a_l.wait_recv()
    near = row_a(y1).at[1]
    a_l = copy(near, near, yd)
    b_r.wait_recv()
    near = row_b(x3).at[0]
    b_r = copy(near, near, xr)
    b_l.wait_recv()
    near = row_b(x1).at[1]
    b_l = copy(near, near, xl)

    ring_xn.advance()
    ring_dy.advance()

    for c in (a_r, a_l, b_r, b_l):
        c.wait_recv()

    def weights(m, cols):
        return wg[lax.div(m, 4), lo(hi(m)), lo(m), :, :, :, cols].reshape(512, -1)

    qkv_cols = slice(0, 3 * HS)
    out_cols = slice(3 * HS, 4 * HS)

    def forward(ref, into, cols, first, step, count):
        def body(i, carry):
            m = ring8(first + step * i)
            w = weights(m, cols)
            for s in range(2):
                into[s] += dot(ref[m, s], w)
            return carry

        lax.fori_loop(0, count, body, 0)

    def forward_dy(*which):
        ring_dy.settle()
        forward(dy, aa, out_cols, *which)

    def forward_xn(*which):
        ring_xn.settle()
        forward(xn, aq, qkv_cols, *which)

    forward_dy(-2, 1, 5)
    forward_xn(-1, 1, 3)
    ring_xn.advance()
    forward_xn(-2, 4, 2)
    ring_dy.advance()
    forward_dy(-3, 6, 2)
    ring_xn.advance()
    forward_xn(-3, 6, 2)
    forward_dy(4, 0, 1)
    forward_xn(4, 0, 1)

    for s in range(2):
        for a in range(3):
            sb[a, s] = aq[s, :, a * HS : (a + 1) * HS].astype(BF)
        sb[3, s] = aa[s].astype(BF)

    def patch_rows(at):
        return pl.ds(pl.multiple_of(at * 32, 32), 32)

    trips = []
    for k in range(1, 8):
        to = lax.rem(tm + k, 8)
        trips.append(copy(sb.at[:, :, patch_rows(to)], rb.at[:, :, tm], along_tm(k)))
    rb[:, :, tm] = sb[:, :, patch_rows(tm), :]
    for c in trips:
        c.wait_recv()

    row_id = lax.broadcasted_iota(jnp.int32, (256, 256), 0)
    col_id = lax.broadcasted_iota(jnp.int32, (256, 256), 1)
    seen = ((row_id & 31) == (col_id & 31)) & ((row_id >> 5) >= (col_id >> 5))
    scale = HS ** (-0.5)
    for s in range(2):
        q, k, v, a = (rb[i, s].reshape(256, HS) for i in range(4))
        scores = jnp.where(seen, dot_t(q, k) * scale, -1e30)
        expo = jnp.exp(scores - jnp.max(scores, axis=1, keepdims=True))
        soft = expo / jnp.sum(expo, axis=1, keepdims=True)
        soft_b = soft.astype(BF)
        dsoft = dot_t(a, v)
        dscore = soft * (dsoft - jnp.sum(dsoft * soft, axis=1, keepdims=True)) * scale
        dscore_b = dscore.astype(BF)
        results = (
            dot(soft_b, v),
            dot(dscore_b, k),
            dot(dscore.T.astype(BF), q),
            dot(soft.T.astype(BF), a),
        )
        for i, value in enumerate(results):
            ob[i, s] = value.astype(BF).reshape(8, 32, HS)

    trips = []
    for k in range(1, 8):
        to = lax.rem(tm + k, 8)
        trips.append(copy(ob.at[:, :, to], gb.at[:, :, patch_rows(tm)], along_tm(k)))
    gb[:, :, patch_rows(tm), :] = ob[:, :, tm]
    for c in trips:
        c.wait_recv()

    for s in range(2):
        for a in range(3):
            gc[s, :, a * HS : (a + 1) * HS] = gb[1 + a, s]

    def input_grad(index, offset):
        m = ring8(offset)
        w = weights(m, qkv_cols)
        ps[index] = dot_t(gc[other], w).astype(BF)
        po[index] = dot_t(gc[core], w)
        return copy(ps.at[index], sr.at[index], sibling)

    def total_of(index, rows):
        return po[index, rows, :] + sr[index, rows, :].astype(F32)

    offsets = (4, 3, -3, 2, -2, 1, -1, 0)
    across = [input_grad(i, offsets[i]) for i in range(3)]

    for s in range(2):
        for a in range(4):
            source = gb[(a + 1) % 4, s]
            gt[a * HS : (a + 1) * HS, s * 256 : (s + 1) * 256] = source.astype(F32).T.astype(BF)

    def weight_grad(yh_at, s_at, xh_at):
        m = (yh_at * 2 + s_at) * 2 + xh_at
        first = dot(gt[: 3 * HS, :], xn[m].reshape(512, 512)).astype(BF)
        second = dot(gt[3 * HS :, :], dy[m].reshape(512, 512)).astype(BF)
        for i in range(4):
            cols = slice(i * HS, (i + 1) * HS)
            wt[yh_at, s_at, xh_at, i // 2, i % 2, : 3 * HS, :] = first[:, cols]
            wt[yh_at, s_at, xh_at, i // 2, i % 2, 3 * HS :, :] = second[:, cols]

    def far_grads(i, carry):
        weight_grad(1 - yh, 0, i)
        weight_grad(i, 1, 1 - xh)
        return carry

    lax.fori_loop(0, 2, far_grads, 0)

    class Scatter:
        def __init__(self, part, right, left, got, tmp, at):
            self.part = part
            self.right = right
            self.left = left
            self.got = got
            self.tmp = tmp
            self.at = at

        def begin(self):
            _, _, two, _ = self.at
            self.r2 = copy(self.part(two, 0), self.got.at[0], self.right)
            self.l2 = copy(self.part(two, 1), self.got.at[1], self.left)

        def near(self):
            _, one, _, three = self.at
            self.r1 = copy(self.part(one, 1), self.got.at[2], self.right)
            self.l1 = copy(self.part(three, 0), self.got.at[3], self.left)

        def chain(self):
            _, one, _, three = self.at
            self.r2.wait_recv()
            self.tmp[0] = (self.part(one, 0)[...].astype(F32) + self.got[0].astype(F32)).astype(BF)
            self.r3 = copy(self.tmp.at[0], self.got.at[4], self.right)
            self.l2.wait_recv()
            self.tmp[1] = (self.part(three, 1)[...].astype(F32) + self.got[1].astype(F32)).astype(BF)
            self.l3 = copy(self.tmp.at[1], self.got.at[5], self.left)

        def finish(self):
            here = self.at[0]
            got = self.got
            self.l1.wait_recv()
            self.r3.wait_recv()
            first = self.part(here, 0)[...].astype(F32) + got[3].astype(F32) + got[4].astype(F32)
            self.r1.wait_recv()
            self.l3.wait_recv()
            second = self.part(here, 1)[...].astype(F32) + got[2].astype(F32) + got[5].astype(F32)
            return first, second

    xs, ys = (x, x1, x2, x3), (y, y1, y2, y3)
    sc_a = Scatter(
        lambda v, half: wt.at[hi(v), 0, half, :, lo(v)], yr, yd, ra.at[0], ta.at[0], ys
    )
    sc_b = Scatter(
        lambda v, half: wt.at[half, 1, hi(v), lo(v), :], xr, xl, ra.at[1], ta.at[1], xs
    )
    sc_a.begin()
    sc_b.begin()

    way_r = ((4, 0), (3, 1), (3, 0), (2, 1), (2, 0), (1, 1), (1, 0))
    way_l = ((4, 1), (3, 0), (3, 1), (2, 0), (2, 1), (1, 0), (1, 1))
    flying = {}

    def hop(direction, order):
        way, sign, to = ((way_r, 1, zr), (way_l, -1, zl))[direction]
        distance, half = way[order]
        offset = sign * distance if distance < 4 else 4
        index = offsets.index(offset)
        rows = slice(half * 128, half * 128 + 128)
        value = total_of(index, rows)
        before = (distance + 1, half)
        if before in way:
            prior = way.index(before)
            flying[direction, prior].wait_recv()
            value = value + cr[direction, prior].astype(F32)
        cs[direction, order] = value.astype(BF)
        flying[direction, order] = copy(cs.at[direction, order], cr.at[direction, order], to)

    across += [input_grad(i, offsets[i]) for i in range(3, 8)]
    for i in range(3):
        across[i].wait_recv()
    for order in range(2):
        hop(0, order)
        hop(1, order)

    def near_grads(i, carry):
        weight_grad(yh, 0, i)
        weight_grad(i, 1, xh)
        return carry

    lax.fori_loop(0, 2, near_grads, 0)
    sc_a.near()
    sc_b.near()

    for s in range(2):
        prod = jnp.zeros((256, HS), F32)
        for a in range(3):
            prod = prod + gb[1 + a, s].astype(F32) * sb[a, s].astype(F32)
        ts[s] = jnp.broadcast_to(jnp.sum(prod.T, axis=0, keepdims=True), (8, 256))
    inner_pair = copy(ts.at[other], tr, sibling)

    for i in range(3, 8):
        across[i].wait_recv()
    hop(0, 2)
    hop(1, 2)
    inner_pair.wait_recv()
    tl[...] = ts[core] + tr[...]
    tt[mp] = tl[...]
    inner = [copy(tl, tt.at[mp], along_z(k)) for k in range(1, 8)]
    sc_a.chain()
    sc_b.chain()
    for order in (3, 4):
        hop(0, order)
        hop(1, order)

    sc2 = []
    for index, (sc, right, left, at) in enumerate(((sc_a, xr, xl, xs), (sc_b, yr, yd, ys))):
        first, second = sc.finish()
        r1[index, 0] = first.astype(BF)
        r1[index, 1] = second.astype(BF)

        def part(v, half, index=index):
            return r1.at[index, hi(v), lo(v), pl.ds(half * 256, 256)]

        stage = Scatter(part, right, left, rc.at[index], tc.at[index], at)
        stage.begin()
        stage.near()
        sc2.append(stage)

    for order in (5, 6):
        hop(0, order)
        hop(1, order)
    for stage in sc2:
        stage.chain()
    for index, stage in enumerate(sc2):
        first, second = stage.finish()
        rf[index, 0:256, :] = first
        rf[index, 256:512, :] = second
    fs[...] = rf[other].astype(BF)
    last = copy(fs, fr, sibling)
    fh[core] = rf[core]

    for c in inner:
        c.wait_recv()
    inner_row = tt[0]
    for k in range(1, 8):
        inner_row = inner_row + tt[k]
    inner_col = jnp.broadcast_to(inner_row[0:1, :] / 4096.0, (HS, 256)).T
    for direction, order in ((0, 5), (0, 6), (1, 5), (1, 6)):
        flying[direction, order].wait_recv()
    for half in range(2):
        rows = slice(half * 128, half * 128 + 128)
        grad = total_of(7, rows)
        for direction, way in enumerate((way_r, way_l)):
            grad = grad + cr[direction, way.index((1, half))].astype(F32)
        inverse = iv[rows, :]
        back = inverse * inverse * inner_col[rows, :]
        for g in range(4):
            cols = slice(g * HS, (g + 1) * HS)
            scaled = grad[:, cols] * gain_ref[:, cols].astype(F32)
            branch = inverse * scaled - x_ref[rows, cols].astype(F32) * back
            gf_ref[rows, cols] = (dy_ref[rows, cols].astype(F32) + branch).astype(BF)

    last.wait_recv()
    fh[other] = fr[...].astype(F32)
    for h in range(2):
        cols = slice(h * HS, (h + 1) * HS)
        for a, ref in enumerate((gq_ref, gk_ref, gv_ref)):
            ref[:, cols] = fh[h, a * HS : (a + 1) * HS, :].T
        go_ref[cols, :] = fh[h, 3 * HS :, :]

    for c in copy.started:
        c.wait_send()


def local(spans, frame_span, norm_gain, w_query, w_key, w_value, w_out, grad_out):
    chosen = frame_span[0, 0] == 0
    frames = jnp.where(chosen, spans[0, 0], spans[0, 1])
    vmem = pl.BlockSpec(memory_space=pltpu.VMEM)
    shape = jax.ShapeDtypeStruct
    scratch = [
        ((8, 2, 256, 512), BF),
        ((8, 2, 256, 512), BF),
        ((2, 128, 512), BF),
        ((2, 2, 2, 2, 2, 128, 512), BF),
        ((8, 8, 256), F32),
        ((8, 256), F32),
        ((256, 128), F32),
        ((2, 256, 384), F32),
        ((2, 256, 128), F32),
        ((4, 2, 256, 128), BF),
        ((4, 2, 8, 32, 128), BF),
        ((4, 2, 8, 32, 128), BF),
        ((4, 2, 256, 128), BF),
        ((2, 256, 384), BF),
        ((512, 512), BF),
        ((2, 8, 256), F32),
        ((8, 256), F32),
        ((8, 256), F32),
        ((8, 8, 256), F32),
        ((8, 256, 512), BF),
        ((8, 256, 512), BF),
        ((8, 256, 512), F32),
        ((2, 7, 128, 512), BF),
        ((2, 7, 128, 512), BF),
        ((2, 2, 2, 2, 2, 512, 128), BF),
        ((2, 6, 2, 512, 128), BF),
        ((2, 2, 2, 512, 128), BF),
        ((2, 2, 2, 512, 128), BF),
        ((2, 6, 256, 128), BF),
        ((2, 2, 256, 128), BF),
        ((2, 512, 128), F32),
        ((512, 128), BF),
        ((512, 128), BF),
        ((2, 512, 128), F32),
    ]
    grad_frames, grad_q, grad_k, grad_v, grad_o = pl.pallas_call(
        kernel,
        out_shape=(
            shape((256, 512), BF),
            shape((128, 256), F32),
            shape((128, 256), F32),
            shape((128, 256), F32),
            shape((256, 128), F32),
        ),
        in_specs=[vmem] * 7,
        out_specs=(vmem,) * 5,
        scratch_shapes=[pltpu.VMEM(*each) for each in scratch]
        + [pltpu.SemaphoreType.DMA((COPIES,)), pltpu.SemaphoreType.DMA((COPIES,))],
        compiler_params=pltpu.CompilerParams(
            collective_id=0, has_side_effects=True, vmem_limit_bytes=56 * 1024 * 1024
        ),
    )(frames, grad_out[0, 0], norm_gain[None, :], w_query, w_key, w_value, w_out)
    which = jnp.arange(2, dtype=jnp.int32)[:, None, None]
    span_grad = jnp.where(which == frame_span[0, 0], grad_frames[None], jnp.zeros((), BF))
    return span_grad[None], grad_q, grad_k, grad_v, grad_o


def solution(mesh):
    placed = (
        P("dp", "tm", None, "mp"),
        P("dp", "tm"),
        P("mp"),
        P(("dp", "tm"), "mp"),
        P(("dp", "tm"), "mp"),
        P(("dp", "tm"), "mp"),
        P("mp", ("dp", "tm")),
        P("dp", "tm", None, "mp"),
    )
    return jax.shard_map(
        local,
        mesh=mesh,
        in_specs=placed,
        out_specs=(
            P("dp", "tm", None, "mp"),
            P(("dp", "tm"), "mp"),
            P(("dp", "tm"), "mp"),
            P(("dp", "tm"), "mp"),
            P("mp", ("dp", "tm")),
        ),
        check_vma=False,
    )
```

time: 739 us -> 123 us (0.17)
  waiting for transfers between devices: 578 us -> 0 us
  Pallas kernels: 0 us -> 113 us
  matrix products: 42.5 us -> 0 us
  blocking collectives: 31.8 us -> 0 us
  starting transfers between devices: 30.2 us -> 0 us
  local copies, waits for them, and re-layouts: 21.4 us -> 4.76 us
  between operations: 15.1 us -> 1.32 us
  other arithmetic: 16 us -> 3.65 us
    all_gather x6 -> x0, waiting for transfers between devices: 374 us -> none  [the longest x1 82.7 us: local(): lax.all_gather(w_out, ('dp', 'tm'), axis=1, tiled=True)]
    unnamed x9 -> x0, waiting for transfers between devices: 193 us -> none
    pallas_call x0 -> x1, Pallas kernels: none -> 113 us  [local(): pl.pallas_call(kernel, out_shape=(shape((256, 512), BF), shape((128, 256)...]
    dot_general x15 -> x0, matrix products: 40.8 us -> none  [the longest x3 9.02 us: local(): jnp.dot(columns, weight_piece, preferred_element_type=jnp.float32)]
    all_to_all x7 -> x0, starting transfers between devices: 29.7 us -> none  [the longest x1 5.02 us: local(): lax.all_to_all(key_rows.reshape(shape5), 'tm', split_axis=2, concat_axis=...]
    all_gather x1 -> x0, blocking collectives: 21.7 us -> none  [local(): lax.all_gather(norm_gain, 'mp', axis=0, tiled=True)]
    unnamed x24 -> x14, local copies, waits for them, and re-layouts: 17.1 us -> 4.18 us
    all_to_all x1 -> x0, blocking collectives: 10.2 us -> none  [local(): lax.all_to_all(patch_att, 'tm', split_axis=1, concat_axis=2, tiled=True)]
  transfers between devices with their start and end apart: 15 -> 0, of which waited for: 11 -> 0; matrix products, arithmetic and copies ran while one was open for 8% -> 0% of each run, Pallas kernels for 0% -> 0%
where the time goes in v1:
time: 123 us
  Pallas kernels  113 us (92%)
  local copies, waits for them, and re-layouts  4.76 us (4%)
  other arithmetic  3.65 us (3%)
  between operations  1.32 us (1%)
    pallas_call x1, Pallas kernels, local(): pl.pallas_call(kernel, out_shape=(shape((256, 512), BF), shape((128, 256)...  113 us
    unnamed x14, local copies, waits for them, and re-layouts  4.18 us

profile of v1, /device:TPU:1, one launch (start us, length us, event | category | flops | bytes accessed | tf_op | source)
XLA Modules:
  0.0 122.8 jit_solution(11596286262892872477)
XLA Ops:
  1.3 0.0 copy-start.4
  1.3 0.7 copy-done.4
  2.0 0.6 broadcast_in_dim.27.gain_ref
  2.6 1.8 %select_bitcast_fusion.x_ref = bf16[256,512]{1,0:T(8,128)(2,1)} fusion(bf16[1,2,256,512]{3,2,1,0:T(8,128)(2,1)} %param.8, pred[]{:T(512)S(6)} %eq.16), kind=kLoop, calls=%fused_computation.1 | loop fusion | flops 131072 | bytes 786433 | tf_op jit(solution)/shard_map/jit(_where)/select_n | solution.py:566
  4.3 113.0 %shard_map.119 = (bf16[256,512]{1,0:T(8,128)(2,1)}, f32[128,256]{1,0:T(8,128)}, f32[128,256]{1,0:T(8,128)}, f32[128,256]{1,0:T(8,128)}, f32[256,128]{1,0:T(8,128)}) custom-call(bf16[256,512]{1,0:T(8,128)(2,1)} %select_bitcast_fusion.x_ref, bf16[256,512]{1,0:T(8,128)(2,1)} %bitcast.6, bf16[1,512]{1,0:T(2,128)(2,1)} %broadcast_in_dim.27.gain_ref, ...), custom_call_target="tpu_custom_call" | custom-call | tf_op jit(solution)/shard_map/pallas_call | solution.py:605
  117.4 0.0 copy-start.3
  117.4 1.9 %broadcast_select_fusion = bf16[1,2,256,512]{3,2,1,0:T(8,128)(2,1)} fusion(pred[2]{0:T(512)(128)(4,1)S(1)} %iota_compare_fusion, bf16[256,512]{1,0:T(8,128)(2,1)} %get-tuple-element.10), kind=kLoop, calls=%fused_computation | loop fusion | flops 262144 | bytes 786434 | tf_op jit(solution)/shard_map/jit(_where)/select_n | solution.py:623
  119.3 0.0 copy-done.3
  119.3 0.0 copy-start.2
  119.3 0.7 copy.18
  119.9 0.3 copy-done.2
  120.2 0.0 copy-start.1
  120.2 0.7 copy.19
  120.9 0.3 copy-done.1
  121.2 0.0 copy-start
  121.2 0.7 copy.20
  121.8 0.3 copy-done
  122.1 0.7 copy.21
  (1 shorter events, 0.0 us)
Async XLA Ops:
  1.3 0.7 copy-start.4
  117.4 1.9 %copy-start.3 = (f32[128,256]{1,0:T(8,128)S(1)}, f32[128,256]{1,0:T(8,128)}, u32[]{:S(2)}) copy-start(f32[128,256]{1,0:T(8,128)} %get-tuple-element.21) | copy-start | bytes 393220
  119.3 1.0 copy-start.2
  120.2 1.0 copy-start.1
  121.2 1.0 copy-start

commit v2 on v1

v2 whole, which is shorter than its diff:
```python
import jax
import jax.numpy as jnp
from jax import lax
from jax.experimental import pallas as pl
from jax.experimental.pallas import tpu as pltpu
from jax.sharding import PartitionSpec as P

HS = 128
EPSILON = 1e-05
BF = jnp.bfloat16
F32 = jnp.float32
MESH = pl.DeviceIdType.MESH
COPIES = 230

ROWS_COLS = (((1,), (1,)), ((), ()))


def dot(left, right):
    return jnp.dot(left, right, preferred_element_type=F32)


def dot_t(left, right):
    return lax.dot_general(left, right, ROWS_COLS, preferred_element_type=F32)


class Copies:
    def __init__(self, send, recv):
        self.send = send
        self.recv = recv
        self.started = []

    def __call__(self, src, dst, device):
        at = len(self.started)
        assert at < COPIES
        copy = pltpu.make_async_remote_copy(
            src_ref=src,
            dst_ref=dst,
            send_sem=self.send.at[at],
            recv_sem=self.recv.at[at],
            device_id=device,
            device_id_type=MESH,
        )
        copy.start()
        self.started.append(copy)
        return copy


def kernel(
    spans_ref,
    which_ref,
    gain_ref,
    wq_ref,
    wk_ref,
    wv_ref,
    wo_ref,
    dy_ref,
    span_out,
    q_out,
    k_out,
    v_out,
    o_out,
    sp,
    xs_in,
    xn,
    dy,
    wl,
    wol,
    wp,
    wg,
    ss,
    sl,
    iv,
    aq,
    aa,
    sb,
    rb,
    so,
    st,
    ob,
    gb,
    gc,
    gt,
    ts,
    tr,
    tl,
    tt,
    ps,
    sr,
    po,
    cs,
    cr,
    wt,
    ra,
    ta,
    r1,
    rc,
    tc,
    rf,
    fs,
    fr,
    fh,
    span_v,
    g_v,
    o_v,
    send,
    recv,
    near_sem,
):
    dp = lax.axis_index("dp")
    tm = lax.axis_index("tm")
    mp = lax.axis_index("mp")
    core = lax.rem(dp, 2)
    other = 1 - core
    yh = lax.div(dp, 2)
    x = lax.div(tm, 2)
    yl = lax.rem(tm, 2)
    y = yh * 2 + yl

    def hi(v):
        return lax.div(v, 2)

    def lo(v):
        return lax.rem(v, 2)

    def device(x_at, y_at):
        return (hi(y_at) * 2 + core, x_at * 2 + lo(y_at), mp)

    def ring8(offset):
        return lax.rem(mp + offset + 8, 8)

    def along_z(offset):
        return (dp, tm, ring8(offset))

    def along_tm(offset):
        return (dp, lax.rem(tm + offset, 8), mp)

    sibling = (yh * 2 + other, tm, mp)
    zr, zl = along_z(1), along_z(-1)
    xs = tuple(lax.rem(x + k, 4) for k in range(4))
    ys = tuple(lax.rem(y + k, 4) for k in range(4))
    xh = hi(x)
    xr, xl = device(xs[1], y), device(xs[3], y)
    yr, yd = device(x, ys[1]), device(x, ys[3])
    far_y = device(x, lax.rem(y + 3 + 2 * yl, 4))

    fetched = []

    def fetch(src, dst):
        c = pltpu.make_async_copy(src, dst, near_sem.at[len(fetched)])
        c.start()
        fetched.append(c)
        return c

    span_in = fetch(spans_ref.at[0], sp)
    w_in = [fetch(ref, wl.at[a]) for a, ref in enumerate((wq_ref, wk_ref, wv_ref))]
    w_in.append(fetch(wo_ref, wol))
    dy_in = fetch(dy_ref.at[0, 0], dy.at[mp, core])

    barrier = pltpu.get_barrier_semaphore()
    partners = [sibling, far_y]
    partners += [along_z(k) for k in range(1, 8)]
    partners += [along_tm(k) for k in range(1, 8)]
    for partner in partners:
        pl.semaphore_signal(barrier, inc=1, device_id=partner, device_id_type=MESH)

    which = which_ref[0, 0]
    gain = gain_ref[...].astype(F32)
    span_in.wait()
    xs_in[...] = jnp.where(which == 0, sp[0], sp[1])
    sums = jnp.zeros((256, HS), F32)
    for g in range(4):
        part = xs_in[:, g * HS : (g + 1) * HS].astype(F32)
        sums = sums + part * part
    row = jnp.sum(sums.T, axis=0, keepdims=True)
    sl[...] = jnp.broadcast_to(row, (8, 256))
    for c in w_in:
        c.wait()
    for h in range(2):
        for a in range(3):
            wp[h, :, a * HS : (a + 1) * HS] = wl[a, :, h * HS : (h + 1) * HS]
        wp[h, :, 3 * HS :] = wol[h * HS : (h + 1) * HS, :].astype(F32).T.astype(BF)
    dy_in.wait()

    pl.semaphore_wait(barrier, len(partners))

    copy = Copies(send, recv)

    gather_ways = (
        (((1, 0), (1, 1), (2, 0), (2, 1), (3, 0), (3, 1), (4, 0)), -1, zr),
        (((1, 1), (1, 0), (2, 1), (2, 0), (3, 1), (3, 0), (4, 1)), 1, zl),
    )

    class Ring:
        def __init__(self, ref):
            self.ref = ref
            self.flight = {}
            home = ref.at[mp, core]
            self.home = home
            self.pending = []

        def begin(self):
            for j in range(2):
                self.pass_on(0, j)
                self.pass_on(1, j)
            self.pending.append(copy(self.home, self.home, sibling))

        def pass_on(self, d, j):
            way, sign, to = gather_ways[d]
            k, half = way[j]
            part = self.ref.at[ring8(sign * (k - 1)), core, pl.ds(half * 128, 128)]
            self.flight[d, j] = copy(part, part, to)

        def take(self, j, forward=True):
            for d in range(2):
                way, sign, _ = gather_ways[d]
                k, half = way[j]
                self.flight[d, j].wait_recv()
                if forward and j + 2 < 7:
                    self.pass_on(d, j + 2)
                part = self.ref.at[ring8(sign * k), core, pl.ds(half * 128, 128)]
                self.pending.append(copy(part, part, sibling))

        def settle(self):
            for c in self.pending:
                c.wait_recv()
            self.pending = []

    class Spread:
        def __init__(self, at, ring, right, left):
            self.at = at
            self.ring = ring
            self.to = (right, left)
            own = at(ring[0])
            self.r = copy(own, own, right)
            self.l = copy(own, own, left)

        def relay(self):
            self.r.wait_recv()
            part = self.at(self.ring[3]).at[pl.ds(0, 64)]
            self.r = copy(part, part, self.to[0])
            self.l.wait_recv()
            part = self.at(self.ring[1]).at[pl.ds(64, 64)]
            self.l = copy(part, part, self.to[1])

        def done(self):
            self.r.wait_recv()
            self.l.wait_recv()

    ring_dy = Ring(dy)
    ring_xn = Ring(xn)

    sumsq = [copy(sl, ss.at[mp], along_z(k)) for k in range(1, 8)]
    mine = wg.at[yh, core, xh, lo(x), yl]
    pair = copy(wp.at[other], mine, sibling)
    ring_dy.begin()
    ss[mp] = sl[...]
    wg[yh, core, xh, lo(x), yl] = wp[core]
    aq[...] = jnp.zeros_like(aq)
    aa[...] = jnp.zeros_like(aa)

    def block(x_at, y_at, s):
        return wg.at[hi(y_at), s, hi(x_at), lo(x_at), lo(y_at)]

    def spread_a(k):
        return Spread(lambda v: block(xs[k], v, 0), ys, yr, yd)

    def spread_b(k):
        return Spread(lambda v: block(v, ys[k], 1), xs, xr, xl)

    pair.wait_recv()
    a1 = Spread(lambda v: block(v, y, 0), xs, xr, xl)
    b1 = Spread(lambda v: block(x, v, 1), ys, yr, yd)
    second = {0: (spread_a(0), spread_b(0))}

    for c in sumsq:
        c.wait_recv()
    total = ss[0]
    for k in range(1, 8):
        total = total + ss[k]
    inv_row = lax.rsqrt(total / 4096.0 + EPSILON)
    iv[...] = jnp.broadcast_to(inv_row[0:1, :], (HS, 256)).T
    for g in range(4):
        cols = slice(g * HS, (g + 1) * HS)
        xn[mp, core, :, cols] = (
            xs_in[:, cols].astype(F32) * iv[...] * gain[:, cols]
        ).astype(BF)
    ring_xn.begin()

    a1.relay()
    b1.relay()
    for k in (3, 1):
        second[k] = (spread_a(k), spread_b(k))

    def relay(k):
        second[k][0].relay()
        second[k][1].relay()

    relay(0)
    ring_xn.take(0)
    a1.done()
    b1.done()
    second[2] = (spread_a(2), spread_b(2))
    ring_dy.take(0, forward=False)
    ring_dy.take(1, forward=False)
    ring_xn.take(1)
    relay(3)
    ring_xn.take(2)
    relay(1)
    ring_xn.take(3)
    relay(2)
    ring_xn.take(4)
    for j in (2, 3):
        ring_dy.pass_on(0, j)
        ring_dy.pass_on(1, j)
    ring_xn.take(5)
    for k in range(4):
        second[k][0].done()
        second[k][1].done()

    def weights(m, cols):
        return wg[lax.div(m, 4), lo(hi(m)), lo(m), :, :, :, cols].reshape(512, -1)

    qkv_cols = slice(0, 3 * HS)
    out_cols = slice(3 * HS, 4 * HS)

    def forward(ref, into, cols, first, step, count):
        def body(i, carry):
            m = ring8(first + step * i)
            w = weights(m, cols)
            for s in range(2):
                into[s] += dot(ref[m, s], w)
            return carry

        lax.fori_loop(0, count, body, 0)

    def forward_dy(*which_chunks):
        ring_dy.settle()
        forward(dy, aa, out_cols, *which_chunks)

    def forward_xn(*which_chunks):
        ring_xn.settle()
        forward(xn, aq, qkv_cols, *which_chunks)

    forward_xn(-2, 1, 5)
    ring_xn.take(6)
    forward_xn(-3, 6, 2)
    forward_xn(4, 0, 1)

    def patch_rows(at):
        return pl.ds(pl.multiple_of(at * 32, 32), 32)

    def swap_out(first, count):
        arrays = pl.ds(first, count)
        trips = []
        for k in range(1, 8):
            to = lax.rem(tm + k, 8)
            trips.append(
                copy(sb.at[arrays, :, patch_rows(to)], rb.at[arrays, :, tm], along_tm(k))
            )
        rb[arrays, :, tm] = sb[arrays, :, patch_rows(tm), :]
        return trips

    def swap_back(first, count):
        arrays = pl.ds(first, count)
        trips = []
        for k in range(1, 8):
            to = lax.rem(tm + k, 8)
            trips.append(
                copy(ob.at[arrays, :, to], gb.at[arrays, :, patch_rows(tm)], along_tm(k))
            )
        gb[arrays, :, patch_rows(tm), :] = ob[arrays, :, tm]
        return trips

    def arrive(trips):
        for c in trips:
            c.wait_recv()

    for s in range(2):
        for a in range(3):
            sb[a, s] = aq[s, :, a * HS : (a + 1) * HS].astype(BF)
    trips = swap_out(0, 3)

    ring_dy.take(2)
    forward_dy(-1, 1, 3)
    ring_dy.take(3)
    arrive(trips)

    row_id = lax.broadcasted_iota(jnp.int32, (256, 256), 0)
    col_id = lax.broadcasted_iota(jnp.int32, (256, 256), 1)
    seen = ((row_id & 31) == (col_id & 31)) & ((row_id >> 5) >= (col_id >> 5))
    scale = HS ** (-0.5)
    for s in range(2):
        q, k, v = (rb[i, s].reshape(256, HS) for i in range(3))
        scores = jnp.where(seen, dot_t(q, k) * scale, -1e30)
        expo = jnp.exp(scores - jnp.max(scores, axis=1, keepdims=True))
        soft = expo / jnp.sum(expo, axis=1, keepdims=True)
        so[s] = soft
        st[s] = soft.T.astype(BF)
        ob[0, s] = dot(soft.astype(BF), v).astype(BF).reshape(8, 32, HS)
    att_trips = swap_back(0, 1)

    forward_dy(-2, 4, 2)
    ring_dy.take(4)
    ring_dy.take(5)
    forward_dy(-3, 6, 2)
    ring_dy.take(6)
    forward_dy(4, 0, 1)

    for s in range(2):
        sb[3, s] = aa[s].astype(BF)
    trips = swap_out(3, 1)

    def keep_transposed(a):
        for s in range(2):
            source = gb[(a + 1) % 4, s]
            gt[a * HS : (a + 1) * HS, s * 256 : (s + 1) * 256] = source.astype(F32).T.astype(BF)

    def spread_columns(value, yh_at, s_at, xh_at, rows):
        for i in range(4):
            wt[yh_at, s_at, xh_at, i // 2, i % 2, rows, :] = value[:, i * HS : (i + 1) * HS]

    def out_grad(m, carry):
        value = dot(gt[3 * HS :, :], dy[m].reshape(512, 512)).astype(BF)
        spread_columns(value, lax.div(m, 4), lo(hi(m)), lo(m), out_cols)
        return carry

    arrive(att_trips)
    keep_transposed(3)
    arrive(trips)
    for s in range(2):
        q, k, v, a = (rb[i, s].reshape(256, HS) for i in range(4))
        soft = so[s]
        dsoft = dot_t(a, v)
        dscore = soft * (dsoft - jnp.sum(dsoft * soft, axis=1, keepdims=True)) * scale
        results = (
            dot(dscore.astype(BF), k),
            dot(dscore.T.astype(BF), q),
            dot(st[s], a),
        )
        for i, value in enumerate(results):
            ob[1 + i, s] = value.astype(BF).reshape(8, 32, HS)
    trips = swap_back(1, 3)
    lax.fori_loop(0, 8, out_grad, 0)
    arrive(trips)

    for s in range(2):
        for a in range(3):
            gc[s, :, a * HS : (a + 1) * HS] = gb[1 + a, s]

    def input_grad(index):
        w = weights(ring8(offsets[index]), qkv_cols)
        ps[index] = dot_t(gc[other], w).astype(BF)
        po[index] = dot_t(gc[core], w)
        return copy(ps.at[index], sr.at[index], sibling)

    def total_of(index, rows):
        return po[index, rows, :] + sr[index, rows, :].astype(F32)

    offsets = (4, 3, -3, 2, -2, 1, -1, 0)
    across = [input_grad(0)]

    for a in range(3):
        keep_transposed(a)

    def weight_grad(yh_at, s_at, xh_at):
        m = (yh_at * 2 + s_at) * 2 + xh_at
        value = dot(gt[: 3 * HS, :], xn[m].reshape(512, 512)).astype(BF)
        spread_columns(value, yh_at, s_at, xh_at, qkv_cols)

    def grads(which_chunk):
        def body(i, carry):
            weight_grad(*which_chunk(i))
            return carry

        lax.fori_loop(0, 2, body, 0)

    def half_rows(half):
        return slice(half * 256, half * 256 + 256)

    class Reduce:
        def __init__(self, part, right, left, got, tmp):
            self.part = part
            self.to = (right, left)
            self.got = got
            self.tmp = tmp

        def far(self):
            self.r2 = copy(self.part(2, 0), self.got.at[0], self.to[0])
            self.l2 = copy(self.part(2, 1), self.got.at[1], self.to[1])

        def near(self):
            self.r1 = copy(self.part(1, 1), self.got.at[2], self.to[0])
            self.l1 = copy(self.part(3, 0), self.got.at[3], self.to[1])

        def chain(self):
            self.r2.wait_recv()
            self.tmp[0] = (self.part(1, 0)[...].astype(F32) + self.got[0].astype(F32)).astype(BF)
            self.r3 = copy(self.tmp.at[0], self.got.at[4], self.to[0])
            self.l2.wait_recv()
            self.tmp[1] = (self.part(3, 1)[...].astype(F32) + self.got[1].astype(F32)).astype(BF)
            self.l3 = copy(self.tmp.at[1], self.got.at[5], self.to[1])

        def finish(self):
            got = self.got
            self.l1.wait_recv()
            self.r3.wait_recv()
            first = self.part(0, 0)[...].astype(F32) + got[3].astype(F32) + got[4].astype(F32)
            self.r1.wait_recv()
            self.l3.wait_recv()
            second = self.part(0, 1)[...].astype(F32) + got[2].astype(F32) + got[5].astype(F32)
            return first, second

    def first_stage(axis, k):
        def part_a(j, half):
            at = ys[j]
            return wt.at[hi(at), 0, hi(xs[k]), lo(xs[k]), lo(at), half_rows(half)]

        def part_b(j, half):
            at = xs[j]
            return wt.at[hi(ys[k]), 1, hi(at), lo(at), lo(ys[k]), half_rows(half)]

        part, right, left = ((part_a, yr, yd), (part_b, xr, xl))[axis]
        return Reduce(part, right, left, ra.at[axis, k], ta.at[axis, k])

    def second_stage(axis):
        def part(j, half):
            return r1.at[axis, j, half_rows(half)]

        right, left = ((xr, xl), (yr, yd))[axis]
        return Reduce(part, right, left, rc.at[axis], tc.at[axis])

    stage1 = [[first_stage(axis, k) for k in range(4)] for axis in range(2)]
    stage2 = [second_stage(axis) for axis in range(2)]

    def begin(k):
        for axis in range(2):
            stage1[axis][k].far()
            stage1[axis][k].near()

    def chain(k):
        for axis in range(2):
            stage1[axis][k].chain()

    def finish(k):
        for axis in range(2):
            for half, value in enumerate(stage1[axis][k].finish()):
                r1[axis, k, half_rows(half), :] = value.astype(BF)

    ways = (
        (((4, 0), (3, 1), (3, 0), (2, 1), (2, 0), (1, 1), (1, 0)), 1, zr),
        (((4, 1), (3, 0), (3, 1), (2, 0), (2, 1), (1, 0), (1, 1)), -1, zl),
    )
    flying = {}

    def hop(order):
        for d, (way, sign, to) in enumerate(ways):
            distance, half = way[order]
            offset = sign * distance if distance < 4 else 4
            rows = slice(half * 128, half * 128 + 128)
            value = total_of(offsets.index(offset), rows)
            before = (distance + 1, half)
            if before in way:
                prior = way.index(before)
                flying[d, prior].wait_recv()
                value = value + cr[d, prior].astype(F32)
            cs[d, order] = value.astype(BF)
            flying[d, order] = copy(cs.at[d, order], cr.at[d, order], to)

    def met(*indices):
        for i in indices:
            across[i].wait_recv()

    grads(lambda i: (i, 0, 1 - xh))
    stage1[0][2].far()
    stage1[0][2].near()
    grads(lambda i: (1 - yh, 1, i))
    stage1[1][2].far()
    stage1[1][2].near()
    across += [input_grad(1), input_grad(2)]
    met(0)
    hop(0)
    grads(lambda i: (i, 0, xh))
    grads(lambda i: (yh, 1, i))
    begin(1)
    begin(3)
    met(1, 2)
    hop(1)
    chain(2)
    across += [input_grad(i) for i in range(3, 8)]
    begin(0)
    chain(1)
    chain(3)
    met(3, 4)
    hop(2)

    for s in range(2):
        prod = jnp.zeros((256, HS), F32)
        for a in range(3):
            prod = prod + gb[1 + a, s].astype(F32) * sb[a, s].astype(F32)
        ts[s] = jnp.broadcast_to(jnp.sum(prod.T, axis=0, keepdims=True), (8, 256))
    inner_pair = copy(ts.at[other], tr, sibling)

    finish(2)
    for axis in range(2):
        stage2[axis].far()
    hop(3)
    chain(0)
    inner_pair.wait_recv()
    tl[...] = ts[core] + tr[...]
    tt[mp] = tl[...]
    inner = [copy(tl, tt.at[mp], along_z(k)) for k in range(1, 8)]
    met(5, 6, 7)
    hop(4)
    finish(1)
    finish(3)
    for axis in range(2):
        stage2[axis].near()
    hop(5)
    for axis in range(2):
        stage2[axis].chain()
    hop(6)
    finish(0)
    for axis in range(2):
        for half, value in enumerate(stage2[axis].finish()):
            rf[axis, half_rows(half), :] = value
    fs[...] = rf[other].astype(BF)
    last = copy(fs, fr, sibling)
    fh[core] = rf[core]

    for c in inner:
        c.wait_recv()
    inner_row = tt[0]
    for k in range(1, 8):
        inner_row = inner_row + tt[k]
    inner_col = jnp.broadcast_to(inner_row[0:1, :] / 4096.0, (HS, 256)).T
    for d in range(2):
        for order in (5, 6):
            flying[d, order].wait_recv()
    for half in range(2):
        rows = slice(half * 128, half * 128 + 128)
        grad = total_of(7, rows)
        for d, (way, _, _) in enumerate(ways):
            grad = grad + cr[d, way.index((1, half))].astype(F32)
        inverse = iv[rows, :]
        back = inverse * inverse * inner_col[rows, :]
        for g in range(4):
            cols = slice(g * HS, (g + 1) * HS)
            scaled = grad[:, cols] * gain[:, cols]
            branch = inverse * scaled - xs_in[rows, cols].astype(F32) * back
            value = (dy[mp, core, rows, cols].astype(F32) + branch).astype(BF)
            for j in range(2):
                span_v[j, rows, cols] = jnp.where(which == j, value, jnp.zeros_like(value))
    written = [fetch(span_v, span_out.at[0])]

    last.wait_recv()
    fh[other] = fr[...].astype(F32)
    for h in range(2):
        cols = slice(h * HS, (h + 1) * HS)
        for a in range(3):
            g_v[a, :, cols] = fh[h, a * HS : (a + 1) * HS, :].T
        o_v[cols, :] = fh[h, 3 * HS :, :]
    for a, ref in enumerate((q_out, k_out, v_out)):
        written.append(fetch(g_v.at[a], ref))
    written.append(fetch(o_v, o_out))
    for c in copy.started:
        c.wait_send()
    for c in written:
        c.wait()


def hand_over(*refs):
    for src, dst in zip(refs[:5], refs[5:]):
        dst[...] = src[...]


def local(spans, frame_span, norm_gain, w_query, w_key, w_value, w_out, grad_out):
    vmem = pl.BlockSpec(memory_space=pltpu.VMEM)
    smem = pl.BlockSpec(memory_space=pltpu.SMEM)
    anywhere = pl.BlockSpec(memory_space=pl.ANY)
    shape = jax.ShapeDtypeStruct
    scratch = [
        ((2, 256, 512), BF),
        ((256, 512), BF),
        ((8, 2, 256, 512), BF),
        ((8, 2, 256, 512), BF),
        ((3, 128, 256), BF),
        ((256, 128), BF),
        ((2, 128, 512), BF),
        ((2, 2, 2, 2, 2, 128, 512), BF),
        ((8, 8, 256), F32),
        ((8, 256), F32),
        ((256, 128), F32),
        ((2, 256, 384), F32),
        ((2, 256, 128), F32),
        ((4, 2, 256, 128), BF),
        ((4, 2, 8, 32, 128), BF),
        ((2, 256, 256), F32),
        ((2, 256, 256), BF),
        ((4, 2, 8, 32, 128), BF),
        ((4, 2, 256, 128), BF),
        ((2, 256, 384), BF),
        ((512, 512), BF),
        ((2, 8, 256), F32),
        ((8, 256), F32),
        ((8, 256), F32),
        ((8, 8, 256), F32),
        ((8, 256, 512), BF),
        ((8, 256, 512), BF),
        ((8, 256, 512), F32),
        ((2, 7, 128, 512), BF),
        ((2, 7, 128, 512), BF),
        ((2, 2, 2, 2, 2, 512, 128), BF),
        ((2, 4, 6, 256, 128), BF),
        ((2, 4, 2, 256, 128), BF),
        ((2, 4, 512, 128), BF),
        ((2, 6, 256, 128), BF),
        ((2, 2, 256, 128), BF),
        ((2, 512, 128), F32),
        ((512, 128), BF),
        ((512, 128), BF),
        ((2, 512, 128), F32),
        ((2, 256, 512), BF),
        ((3, 128, 256), F32),
        ((256, 128), F32),
    ]
    out_shape = (
        shape((1, 2, 256, 512), BF),
        shape((128, 256), F32),
        shape((128, 256), F32),
        shape((128, 256), F32),
        shape((256, 128), F32),
    )
    results = pl.pallas_call(
        kernel,
        out_shape=out_shape,
        in_specs=[anywhere, smem, vmem] + [anywhere] * 5,
        out_specs=(anywhere,) * 5,
        scratch_shapes=[pltpu.VMEM(*each) for each in scratch]
        + [pltpu.SemaphoreType.DMA((n,)) for n in (COPIES, COPIES, 16)],
        compiler_params=pltpu.CompilerParams(
            collective_id=0, has_side_effects=True, vmem_limit_bytes=56 * 1024 * 1024
        ),
    )(spans, frame_span, norm_gain[None, :], w_query, w_key, w_value, w_out, grad_out)
    return pl.pallas_call(
        hand_over,
        out_shape=out_shape,
        in_specs=[vmem] * 5,
        out_specs=(vmem,) * 5,
    )(*results)


def solution(mesh):
    placed = (
        P("dp", "tm", None, "mp"),
        P("dp", "tm"),
        P("mp"),
        P(("dp", "tm"), "mp"),
        P(("dp", "tm"), "mp"),
        P(("dp", "tm"), "mp"),
        P("mp", ("dp", "tm")),
        P("dp", "tm", None, "mp"),
    )
    return jax.shard_map(
        local,
        mesh=mesh,
        in_specs=placed,
        out_specs=(
            P("dp", "tm", None, "mp"),
            P(("dp", "tm"), "mp"),
            P(("dp", "tm"), "mp"),
            P(("dp", "tm"), "mp"),
            P("mp", ("dp", "tm")),
        ),
        check_vma=False,
    )
```

time: 123 us -> 108 us (0.88)
  Pallas kernels: 113 us -> 106 us
  local copies, waits for them, and re-layouts: 4.76 us -> 0.59 us
  other arithmetic: 3.65 us -> 0 us
    pallas_call x1 -> x2, Pallas kernels: 113 us -> 106 us  [the longest x1 104 us: local(): pl.pallas_call(kernel, out_shape=out_shape, in_specs=[anywhere, smem, vme...]
    unnamed x14 -> x2, local copies, waits for them, and re-layouts: 4.18 us -> 0.01 us
    select_n x2 -> x0, other arithmetic: 3.65 us -> none  [the longest x1 1.89 us: local(): jnp.where(which == frame_span[0, 0], grad_frames[None], jnp.zeros((), BF))]
where the time goes in v2:
time: 108 us
  Pallas kernels  106 us (98%)
  between operations  1.31 us (1%)
    pallas_call x1, Pallas kernels, local(): pl.pallas_call(kernel, out_shape=out_shape, in_specs=[anywhere, smem, vme...  104 us
    pallas_call x1, Pallas kernels, local(): pl.pallas_call(hand_over, out_shape=out_shape, in_specs=[vmem] * 5, out_s...  2.2 us

profile of v2, /device:TPU:1, one launch (start us, length us, event | category | flops | bytes accessed | tf_op | source)
XLA Modules:
  0.0 107.9 jit_solution(11178536317558117908)
XLA Ops:
  0.6 0.0 copy-start
  1.3 0.0 copy-done
  1.3 0.6 broadcast_in_dim.3.gain_ref
  1.9 103.8 %shard_map.119 = (bf16[1,2,256,512]{3,2,1,0:T(8,128)(2,1)}, f32[128,256]{1,0:T(8,128)}, f32[128,256]{1,0:T(8,128)}, f32[128,256]{1,0:T(8,128)}, f32[256,128]{1,0:T(8,128)}) custom-call(bf16[1,2,256,512]{3,2,1,0:T(8,128)(2,1)} %spans_ref.1, s32[1,1]{1,0:T(1,128)S(6)} %copy.13.which_ref, bf16[1,512]{1,0:T(2,128)(2,1)} %broadcast_in_dim.3.gain_ref, ...), custom_call_target="tpu_custom_call" | custom-call | tf_op jit(solution)/shard_map/pallas_call | solution.py:733
  105.7 2.2 %shard_map.120 = (bf16[1,2,256,512]{3,2,1,0:T(8,128)(2,1)}, f32[128,256]{1,0:T(8,128)}, f32[128,256]{1,0:T(8,128)}, f32[128,256]{1,0:T(8,128)}, f32[256,128]{1,0:T(8,128)}) custom-call(bf16[1,2,256,512]{3,2,1,0:T(8,128)(2,1)} %get-tuple-element.10.refs_0_, f32[128,256]{1,0:T(8,128)} %get-tuple-element.11.refs_1_, f32[128,256]{1,0:T(8,128)} %get-tuple-element.12.refs_2_, ...), custom_call_target="tpu_custom_call" | custom-call | tf_op jit(solution)/shard_map/pallas_call | solution.py:744
Async XLA Ops:
  0.6 0.7 copy-start

commit v3 on v2

v3 whole, which is shorter than its diff:
```python
import math

import jax
import jax.numpy as jnp
from jax import lax
from jax.experimental import pallas as pl
from jax.experimental.pallas import tpu as pltpu
from jax.sharding import PartitionSpec as P

HS = 128
EPSILON = 1e-05
BF = jnp.bfloat16
F32 = jnp.float32
MESH = pl.DeviceIdType.MESH
ARRIVALS = 100
DEPARTURES = 8
RULER = 6144

ROWS_COLS = (((1,), (1,)), ((), ()))


def dot(left, right):
    return jnp.dot(left, right, preferred_element_type=F32)


def dot_t(left, right):
    return lax.dot_general(left, right, ROWS_COLS, preferred_element_type=F32)


class Batch:
    def __init__(self, copies, at):
        self.copies = copies
        self.at = at
        self.kib = 0

    def __call__(self, src, dst, device):
        copies = self.copies
        kib = math.prod(dst.shape) * jnp.dtype(dst.dtype).itemsize // 1024
        if copies.departed[-1] + kib > RULER:
            copies.departed.append(0)
        copies.departed[-1] += kib
        self.kib += kib
        pltpu.make_async_remote_copy(
            src_ref=src,
            dst_ref=dst,
            send_sem=copies.send.at[len(copies.departed) - 1],
            recv_sem=copies.recv.at[self.at],
            device_id=device,
            device_id_type=MESH,
        ).start()

    def wait(self):
        copies = self.copies
        copies.open.remove(self)
        copies.wait(copies.recv.at[self.at], self.kib)


class Copies:
    def __init__(self, send, recv, ruler):
        self.send = send
        self.recv = recv
        self.ruler = ruler
        self.departed = [0]
        self.count = 0
        self.open = []

    def batch(self):
        assert self.count < ARRIVALS
        new = Batch(self, self.count)
        self.count += 1
        self.open.append(new)
        return new

    def __call__(self, src, dst, device):
        new = self.batch()
        new(src, dst, device)
        return new

    def wait(self, sem, kib):
        span = self.ruler.at[pl.ds(0, kib)]
        pltpu.make_async_copy(span, span, sem).wait()

    def finish(self):
        assert not self.open
        assert len(self.departed) <= DEPARTURES
        for at, kib in enumerate(self.departed):
            self.wait(self.send.at[at], kib)


def kernel(
    spans_ref,
    which_ref,
    gain_ref,
    wq_ref,
    wk_ref,
    wv_ref,
    wo_ref,
    dy_ref,
    span_out,
    q_out,
    k_out,
    v_out,
    o_out,
    sp,
    xs_in,
    xn,
    dy,
    wl,
    wol,
    wp,
    wg,
    ss,
    sl,
    iv,
    aq,
    aa,
    sb,
    rb,
    so,
    st,
    ob,
    gb,
    gc,
    gt,
    ts,
    tr,
    tl,
    tt,
    ps,
    sr,
    cs,
    cr,
    wt,
    wt_o,
    ra_o,
    ta_o,
    r1_o,
    rc_o,
    tc_o,
    ra,
    ta,
    r1,
    rc,
    tc,
    rf,
    fs,
    fr,
    fh,
    span_v,
    g_v,
    o_v,
    ruler,
    send,
    recv,
    near_sem,
):
    dp = lax.axis_index("dp")
    tm = lax.axis_index("tm")
    mp = lax.axis_index("mp")
    core = lax.rem(dp, 2)
    other = 1 - core
    yh = lax.div(dp, 2)
    x = lax.div(tm, 2)
    yl = lax.rem(tm, 2)
    y = yh * 2 + yl

    def hi(v):
        return lax.div(v, 2)

    def lo(v):
        return lax.rem(v, 2)

    def device(x_at, y_at):
        return (hi(y_at) * 2 + core, x_at * 2 + lo(y_at), mp)

    def ring8(offset):
        return lax.rem(mp + offset + 8, 8)

    def along_z(offset):
        return (dp, tm, ring8(offset))

    def along_tm(offset):
        return (dp, lax.rem(tm + offset, 8), mp)

    sibling = (yh * 2 + other, tm, mp)
    zr, zl = along_z(1), along_z(-1)
    xs = tuple(lax.rem(x + k, 4) for k in range(4))
    ys = tuple(lax.rem(y + k, 4) for k in range(4))
    xh = hi(x)
    xr, xl = device(xs[1], y), device(xs[3], y)
    yr, yd = device(x, ys[1]), device(x, ys[3])
    far_y = device(x, lax.rem(y + 3 + 2 * yl, 4))

    barrier = pltpu.get_barrier_semaphore()
    partners = [sibling, far_y]
    partners += [along_z(k) for k in range(1, 8)]
    partners += [along_tm(k) for k in range(1, 8)]
    for partner in partners:
        pl.semaphore_signal(barrier, inc=1, device_id=partner, device_id_type=MESH)

    fetched = []

    def fetch(src, dst):
        c = pltpu.make_async_copy(src, dst, near_sem.at[len(fetched)])
        c.start()
        fetched.append(c)
        return c

    span_in = fetch(spans_ref.at[0], sp)
    w_in = [fetch(ref, wl.at[a]) for a, ref in enumerate((wq_ref, wk_ref, wv_ref))]
    w_in.append(fetch(wo_ref, wol))
    dy_in = fetch(dy_ref.at[0, 0], dy.at[mp, core])

    which = which_ref[0, 0]
    gain = gain_ref[...].astype(F32).reshape(1, 512)
    span_in.wait()
    xs_in[...] = jnp.where(which == 0, sp[0], sp[1])
    sums = jnp.zeros((256, HS), F32)
    for g in range(4):
        part = xs_in[:, g * HS : (g + 1) * HS].astype(F32)
        sums = sums + part * part
    row = jnp.sum(sums.T, axis=0, keepdims=True)
    sl[...] = jnp.broadcast_to(row, (8, 256))
    for c in w_in:
        c.wait()
    for h in range(2):
        for a in range(3):
            wp[h, :, a * HS : (a + 1) * HS] = wl[a, :, h * HS : (h + 1) * HS]
        wp[h, :, 3 * HS :] = wol[h * HS : (h + 1) * HS, :].astype(F32).T.astype(BF)
    pl.semaphore_wait(barrier, len(partners))

    copy = Copies(send, recv, ruler)

    halves = (
        ((1, 0, 128), (1, 128, 128), (2, 0, 128), (2, 128, 128), (3, 0, 128), (3, 128, 128), (4, 0, 128)),
        ((1, 128, 128), (1, 0, 128), (2, 128, 128), (2, 0, 128), (3, 128, 128), (3, 0, 128), (4, 128, 128)),
    )
    first_half = ((1, 0, 128), (1, 128, 128), (2, 0, 128), (3, 0, 128))
    staged = (
        first_half
        + ((4, 0, 64), (2, 128, 64), (2, 192, 64))
        + ((3, 128, 64), (3, 192, 64), (4, 128, 64)),
        first_half
        + ((4, 64, 64), (2, 192, 64), (2, 128, 64))
        + ((3, 192, 64), (3, 128, 64), (4, 192, 64)),
    )

    class Ring:
        def __init__(self, ref, ways, src):
            self.ref = ref
            self.ways = ways
            self.src = src
            self.flight = {}
            self.pending = {}

        def part(self, d, k, first, rows):
            offset = -k if d == 0 else k
            return self.ref.at[ring8(offset), core, pl.ds(first, rows)]

        def pass_on(self, d, j):
            k, first, rows = self.ways[d][j]
            part = self.part(d, k - 1, first, rows)
            src = self.src.at[pl.ds(first, rows)] if k == 1 else part
            if d == 0:
                self.flight[j] = copy.batch()
            self.flight[j](src, part, (zr, zl)[d])

        def send(self, *which_parts):
            for j in which_parts:
                for d in range(2):
                    self.pass_on(d, j)

        def take(self, *which_parts, then=()):
            for at, j in enumerate(which_parts):
                self.flight[j].wait()
                if then:
                    self.send(then[at])

        def share(self, *which_parts, half=0):
            for d in range(2):
                rows = [self.ways[d][j] for j in which_parts]
                first = min(r[1] for r in rows)
                part = self.part(d, rows[0][0], first, sum(r[2] for r in rows))
                self.hand(part, half)

        def hand(self, part, half=0):
            if half not in self.pending:
                self.pending[half] = copy.batch()
            self.pending[half](part, part, sibling)

        def settle(self, half=0):
            if half in self.pending:
                self.pending.pop(half).wait()

    grad_in = dy_ref.at[0, 0]
    ring_dy = Ring(dy, staged, grad_in)
    sumsq = copy.batch()
    for k in range(1, 8):
        sumsq(sl, ss.at[mp], along_z(k))
    ss[mp] = sl[...]
    mine = wg.at[yh, core, xh, lo(x), yl]
    pair = copy(wp.at[other], mine, sibling)
    ring_dy.send(0, 1)
    wg[yh, core, xh, lo(x), yl] = wp[core]

    class Spread:
        def __init__(self, at, ring, right, left):
            self.at = at
            self.ring = ring
            self.to = (right, left)
            own = at(ring[0])
            self.trip = copy.batch()
            self.trip(own, own, right)
            self.trip(own, own, left)

        def relay(self):
            self.trip.wait()
            self.trip = copy.batch()
            part = self.at(self.ring[3]).at[pl.ds(0, 64)]
            self.trip(part, part, self.to[0])
            part = self.at(self.ring[1]).at[pl.ds(64, 64)]
            self.trip(part, part, self.to[1])

        def done(self):
            self.trip.wait()

    def block(x_at, y_at, s):
        return wg.at[hi(y_at), s, hi(x_at), lo(x_at), lo(y_at)]

    def spread_a(k):
        return Spread(lambda v: block(xs[k], v, 0), ys, yr, yd)

    def spread_b(k):
        return Spread(lambda v: block(v, ys[k], 1), xs, xr, xl)

    pair.wait()
    a1 = Spread(lambda v: block(v, y, 0), xs, xr, xl)
    b1 = Spread(lambda v: block(x, v, 1), ys, yr, yd)
    second = {0: (spread_a(0), spread_b(0))}

    sumsq.wait()
    total = ss[0]
    for k in range(1, 8):
        total = total + ss[k]
    inv_row = lax.rsqrt(total / 4096.0 + EPSILON)
    iv[...] = jnp.broadcast_to(inv_row[0:1, :], (HS, 256)).T
    for g in range(4):
        cols = slice(g * HS, (g + 1) * HS)
        xn[mp, core, :, cols] = (
            xs_in[:, cols].astype(F32) * iv[...] * gain[:, cols]
        ).astype(BF)
    ring_xn = Ring(xn, halves, xn.at[mp, core])
    ring_xn.send(0, 1)
    ring_xn.hand(xn.at[mp, core])
    ring_dy.take(0, then=(2,))
    aq[...] = jnp.zeros_like(aq)
    aa[...] = jnp.zeros_like(aa)

    a1.relay()
    b1.relay()
    for k in (3, 1):
        second[k] = (spread_a(k), spread_b(k))

    def relay(k):
        second[k][0].relay()
        second[k][1].relay()

    relay(0)
    dy_in.wait()
    ring_dy.hand(dy.at[mp, core, pl.ds(0, 128)], 0)
    ring_dy.hand(dy.at[mp, core, pl.ds(128, 128)], 1)
    ring_dy.take(1)
    ring_dy.share(0)
    ring_dy.share(1, half=1)
    a1.done()
    b1.done()
    second[2] = (spread_a(2), spread_b(2))
    ring_xn.take(0, then=(2,))
    ring_xn.take(1, then=(3,))
    ring_xn.share(0, 1)
    relay(3)
    ring_dy.take(2, then=(3,))
    ring_dy.share(2)
    relay(1)
    ring_xn.take(2, then=(4,))
    relay(2)
    ring_xn.take(3, then=(5,))
    ring_xn.share(2, 3)
    ring_dy.take(3, then=(4,))
    ring_dy.share(3)
    for k in range(4):
        second[k][0].done()
        second[k][1].done()

    def weights(m, cols):
        return wg[lax.div(m, 4), lo(hi(m)), lo(m), :, :, :, cols].reshape(512, -1)

    qkv_cols = slice(0, 3 * HS)
    out_cols = slice(3 * HS, 4 * HS)

    def forward(ref, into, cols, rows, first, step, count):
        def body(i, carry):
            m = ring8(first + step * i)
            shape = (2, rows.stop - rows.start)
            left = ref[m, :, rows].reshape(shape[0] * shape[1], 512)
            into[:, rows] += dot(left, weights(m, cols)).reshape(*shape, -1)
            return carry

        lax.fori_loop(0, count, body, 0)

    def forward_xn(*which_chunks):
        ring_xn.settle()
        forward(xn, aq, qkv_cols, slice(0, 256), *which_chunks)

    def group(half):
        return slice(half * 128, half * 128 + 128)

    def forward_dy(half, *which_chunks):
        ring_dy.settle(half)
        forward(dy, aa, out_cols, group(half), *which_chunks)

    forward_xn(-1, 1, 3)
    ring_xn.take(4, then=(6,))
    ring_dy.send(5, 6)
    forward_dy(0, -1, 1, 3)
    ring_xn.take(5)
    ring_xn.share(4, 5)
    forward_xn(-2, 4, 2)
    ring_dy.take(4)
    ring_dy.hand(dy.at[ring8(4), core, pl.ds(0, 128)])
    forward_dy(0, -2, 4, 2)
    forward_dy(0, -3, 6, 2)
    forward_xn(-3, 6, 2)
    ring_xn.take(6)
    ring_xn.hand(xn.at[ring8(4), core])
    forward_dy(0, 4, 0, 1)

    def strip(at):
        return pl.ds(pl.multiple_of(at * 16, 16), 16)

    def swap_out(arrays, parts):
        trips = copy.batch()
        for k in range(1, 8):
            src = sb.at[arrays, parts, :, strip(lax.rem(tm + k, 8))]
            trips(src, rb.at[arrays, parts, :, tm], along_tm(k))
        rb[arrays, parts, :, tm] = sb[arrays, parts, :, strip(tm), :]
        return trips

    def swap_back(arrays, parts):
        trips = copy.batch()
        for k in range(1, 8):
            dst = gb.at[arrays, parts, :, strip(tm)]
            trips(ob.at[arrays, parts, :, lax.rem(tm + k, 8)], dst, along_tm(k))
        gb[arrays, parts, :, strip(tm), :] = ob[arrays, parts, :, tm]
        return trips

    both = pl.ds(0, 2)
    one = (pl.ds(0, 1), pl.ds(1, 1))

    def grads_out(part):
        for s in range(2):
            sb[3, part, s] = aa[s, group(part)].astype(BF)
        return swap_out(pl.ds(3, 1), one[part])

    away = [grads_out(0)]
    forward_xn(4, 0, 1)
    ring_dy.take(5, then=(7,))
    for s in range(2):
        for a in range(3):
            for part in range(2):
                sb[a, part, s] = aq[s, group(part), a * HS : (a + 1) * HS].astype(BF)
    trips = swap_out(pl.ds(0, 3), both)
    ring_dy.take(6, then=(8,))
    ring_dy.share(5, 6, half=1)
    forward_dy(1, -1, 1, 3)
    ring_dy.take(7, then=(9,))
    forward_dy(1, -2, 4, 2)
    ring_dy.take(8)
    ring_dy.share(7, 8, half=1)
    forward_dy(1, -3, 6, 2)
    ring_dy.take(9)
    ring_dy.hand(dy.at[ring8(4), core, pl.ds(128, 128)], 1)
    forward_dy(1, 4, 0, 1)
    away.append(grads_out(1))
    trips.wait()

    row_id = lax.broadcasted_iota(jnp.int32, (256, 256), 0)
    col_id = lax.broadcasted_iota(jnp.int32, (256, 256), 1)
    same = ((row_id & 15) == (col_id & 15)) & ((row_id >> 7) == (col_id >> 7))
    seen = same & ((row_id >> 4) >= (col_id >> 4))
    scale = HS ** (-0.5)

    def held(i, part):
        return rb[i, part].reshape(256, HS)

    def attend(part):
        q, k, v = (held(i, part) for i in range(3))
        scores = jnp.where(seen, dot_t(q, k) * scale, -1e30)
        expo = jnp.exp(scores - jnp.max(scores, axis=1, keepdims=True))
        soft = expo / jnp.sum(expo, axis=1, keepdims=True)
        so[part] = soft
        st[part] = soft.T.astype(BF)
        ob[0, part] = dot(soft.astype(BF), v).astype(BF).reshape(2, 8, 16, HS)

    def attend_back(part):
        away[part].wait()
        q, k, v, a = (held(i, part) for i in range(4))
        soft = so[part]
        dsoft = dot_t(a, v)
        dscore = soft * (dsoft - jnp.sum(dsoft * soft, axis=1, keepdims=True)) * scale
        results = (
            dot(dscore.astype(BF), k),
            dot(dscore.T.astype(BF), q),
            dot(st[part], a),
        )
        for i, value in enumerate(results):
            ob[1 + i, part] = value.astype(BF).reshape(2, 8, 16, HS)
        return swap_back(pl.ds(1, 3), one[part])

    attend(0)
    back = [attend_back(0)]
    attend(1)
    att_trips = swap_back(pl.ds(0, 1), both)
    back.append(attend_back(1))

    def keep_transposed(a):
        for part in range(2):
            for s in range(2):
                first = s * 256 + part * 128
                source = gb[(a + 1) % 4, part, s].astype(F32)
                gt[a * HS : (a + 1) * HS, first : first + 128] = source.T.astype(BF)

    def out_grad(m, carry):
        value = dot(gt[3 * HS :, :], dy[m].reshape(512, 512)).astype(BF)
        place = wt_o.at[lax.div(m, 4), lo(hi(m)), lo(m)]
        for i in range(4):
            place[i // 2, i % 2] = value[:, i * HS : (i + 1) * HS]
        return carry

    att_trips.wait()
    keep_transposed(3)
    lax.fori_loop(0, 8, out_grad, 0)

    offsets = (4, 3, -3, 2, -2, 1, -1, 0)

    def grads_in(half):
        for s in range(2):
            for a in range(3):
                gc[s, group(half), a * HS : (a + 1) * HS] = gb[1 + a, half, s]

    def input_grads(half, first, last):
        met = copy.batch()
        rows = group(half)
        for index in range(first, last):
            w = weights(ring8(offsets[index]), qkv_cols)
            value = dot_t(gc[:, rows, :].reshape(256, 3 * HS), w).astype(BF)
            ps[index, :, rows, :] = value.reshape(2, 128, 512)
            part = pl.ds(half * 128, 128)
            met(ps.at[index, other, part], sr.at[index, part], sibling)
        across.append(met)

    across = []

    def total_of(index, half):
        rows = group(half)
        return ps[index, core, rows, :].astype(F32) + sr[index, rows, :].astype(F32)

    ways = (((4, 3, 2, 1), (3, 2, 1)), ((3, 2, 1), (4, 3, 2, 1)))
    flying = {}

    def hop(half, order):
        if across and order < 2:
            across.pop().wait()
        if order:
            flying[half].wait()
        flying[half] = copy.batch()
        slot = half * 4 + order
        for d in range(2):
            way = ways[half][d]
            if order >= len(way):
                continue
            distance = way[order]
            offset = 4 if distance == 4 else (distance, -distance)[d]
            value = total_of(offsets.index(offset), half)
            if order:
                value = value + cr[d, slot - 1].astype(F32)
            cs[d, slot] = value.astype(BF)
            flying[half](cs.at[d, slot], cr.at[d, slot], (zr, zl)[d])

    class Reduce:
        def __init__(self, part, right, left, got, tmp):
            self.part = part
            self.to = (right, left)
            self.got = got
            self.tmp = tmp

        def far(self):
            self.first = copy.batch()
            self.first(self.part(2, 0), self.got.at[0], self.to[0])
            self.first(self.part(2, 1), self.got.at[1], self.to[1])

        def near(self):
            self.second = copy.batch()
            self.second(self.part(1, 1), self.got.at[2], self.to[0])
            self.second(self.part(3, 0), self.got.at[3], self.to[1])

        def chain(self):
            self.first.wait()
            for d, (at, half) in enumerate(((1, 0), (3, 1))):
                value = self.part(at, half)[...].astype(F32) + self.got[d].astype(F32)
                self.tmp[d] = value.astype(BF)
                self.second(self.tmp.at[d], self.got.at[4 + d], self.to[d])

        def finish(self):
            got = self.got
            self.second.wait()
            first = self.part(0, 0)[...].astype(F32) + got[3].astype(F32) + got[4].astype(F32)
            second = self.part(0, 1)[...].astype(F32) + got[2].astype(F32) + got[5].astype(F32)
            return first, second

    def out_first(axis):
        def part_a(j, half):
            return wt_o.at[hi(ys[j]), 0, half, :, lo(ys[j])]

        def part_b(j, half):
            return wt_o.at[half, 1, hi(xs[j]), lo(xs[j]), :]

        part, right, left = ((part_a, yr, yd), (part_b, xr, xl))[axis]
        return Reduce(part, right, left, ra_o.at[axis], ta_o.at[axis])

    def out_second(axis):
        ring = (xs, ys)[axis]

        def part(j, half):
            return r1_o.at[axis, hi(ring[j]), lo(ring[j]), pl.ds(half * 64, 64)]

        right, left = ((xr, xl), (yr, yd))[axis]
        return Reduce(part, right, left, rc_o.at[axis], tc_o.at[axis])

    out1 = [out_first(axis) for axis in range(2)]
    out2 = [out_second(axis) for axis in range(2)]
    for stage in out1:
        stage.far()
        stage.near()
    back[0].wait()
    grads_in(0)
    input_grads(0, 0, 3)
    back[1].wait()

    for a in range(3):
        keep_transposed(a)

    def weight_grad(yh_at, s_at, xh_at):
        m = (yh_at * 2 + s_at) * 2 + xh_at
        value = dot(gt[: 3 * HS, :], xn[m].reshape(512, 512)).astype(BF)
        for i in range(4):
            wt[yh_at, s_at, xh_at, i // 2, i % 2] = value[:, i * HS : (i + 1) * HS]

    def grads(which_chunk):
        def body(i, carry):
            weight_grad(*which_chunk(i))
            return carry

        lax.fori_loop(0, 2, body, 0)

    def half_rows(half):
        return slice(half * 192, half * 192 + 192)

    def first_stage(axis, k):
        def part_a(j, half):
            at = ys[j]
            return wt.at[hi(at), 0, hi(xs[k]), lo(xs[k]), lo(at), half_rows(half)]

        def part_b(j, half):
            at = xs[j]
            return wt.at[hi(ys[k]), 1, hi(at), lo(at), lo(ys[k]), half_rows(half)]

        part, right, left = ((part_a, yr, yd), (part_b, xr, xl))[axis]
        return Reduce(part, right, left, ra.at[axis, k], ta.at[axis, k])

    def second_stage(axis):
        def part(j, half):
            return r1.at[axis, j, half_rows(half)]

        right, left = ((xr, xl), (yr, yd))[axis]
        return Reduce(part, right, left, rc.at[axis], tc.at[axis])

    stage1 = [[first_stage(axis, k) for k in range(4)] for axis in range(2)]
    stage2 = [second_stage(axis) for axis in range(2)]

    def begin(k):
        for axis in range(2):
            stage1[axis][k].far()
            stage1[axis][k].near()

    def chain(k):
        for axis in range(2):
            stage1[axis][k].chain()

    def finish(k):
        for axis in range(2):
            for half, value in enumerate(stage1[axis][k].finish()):
                r1[axis, k, half_rows(half), :] = value.astype(BF)

    grads(lambda i: (i, 0, 1 - xh))
    stage1[0][2].far()
    stage1[0][2].near()
    hop(0, 0)
    grads(lambda i: (1 - yh, 1, i))
    stage1[1][2].far()
    stage1[1][2].near()
    grads_in(1)
    input_grads(1, 0, 3)
    grads(lambda i: (i, 0, xh))
    for k in (1, 3):
        stage1[0][k].far()
        stage1[0][k].near()
    hop(1, 0)
    grads(lambda i: (yh, 1, i))
    for k in (1, 3):
        stage1[1][k].far()
        stage1[1][k].near()
    input_grads(0, 3, 8)
    chain(2)
    hop(0, 1)
    begin(0)
    for stage in out1:
        stage.chain()
    input_grads(1, 3, 8)
    chain(1)
    chain(3)
    hop(1, 1)
    finish(2)
    for axis in range(2):
        stage2[axis].far()
    hop(0, 2)
    for axis in range(2):
        for half, value in enumerate(out1[axis].finish()):
            r1_o[axis, half] = value.astype(BF)
        out2[axis].far()
        out2[axis].near()
    chain(0)

    for s in range(2):
        prod = jnp.zeros((256, HS), F32)
        for a in range(3):
            left = jnp.concatenate([gb[1 + a, part, s] for part in range(2)], axis=0)
            right = jnp.concatenate([sb[a, part, s] for part in range(2)], axis=0)
            prod = prod + left.astype(F32) * right.astype(F32)
        ts[s] = jnp.broadcast_to(jnp.sum(prod.T, axis=0, keepdims=True), (8, 256))
    inner_pair = copy(ts.at[other], tr, sibling)

    hop(1, 2)
    for stage in out2:
        stage.chain()
    finish(1)
    finish(3)
    for axis in range(2):
        stage2[axis].near()
    inner_pair.wait()
    tl[...] = ts[core] + tr[...]
    tt[mp] = tl[...]
    inner = copy.batch()
    for k in range(1, 8):
        inner(tl, tt.at[mp], along_z(k))
    hop(0, 3)
    for axis in range(2):
        stage2[axis].chain()
    hop(1, 3)
    finish(0)
    for axis in range(2):
        for half, value in enumerate(out2[axis].finish()):
            rf[axis, 384 + half * 64 : 448 + half * 64, :] = value
        for half, value in enumerate(stage2[axis].finish()):
            rf[axis, half_rows(half), :] = value
    fs[...] = rf[other].astype(BF)
    last = copy(fs, fr, sibling)
    fh[core] = rf[core]

    inner.wait()
    inner_row = tt[0]
    for k in range(1, 8):
        inner_row = inner_row + tt[k]
    inner_col = jnp.broadcast_to(inner_row[0:1, :] / 4096.0, (HS, 256)).T
    for half in range(2):
        rows = group(half)
        flying[half].wait()
        grad = total_of(7, half)
        for d in range(2):
            final = len(ways[half][d]) - 1
            grad = grad + cr[d, half * 4 + final].astype(F32)
        inverse = iv[rows, :]
        back = inverse * inverse * inner_col[rows, :]
        for g in range(4):
            cols = slice(g * HS, (g + 1) * HS)
            scaled = grad[:, cols] * gain[:, cols]
            branch = inverse * scaled - xs_in[rows, cols].astype(F32) * back
            value = (dy[mp, core, rows, cols].astype(F32) + branch).astype(BF)
            for j in range(2):
                span_v[j, rows, cols] = jnp.where(which == j, value, jnp.zeros_like(value))
    written = [fetch(span_v, span_out.at[0])]

    last.wait()
    fh[other] = fr[...].astype(F32)
    for h in range(2):
        cols = slice(h * HS, (h + 1) * HS)
        for a in range(3):
            g_v[a, :, cols] = fh[h, a * HS : (a + 1) * HS, :].T
        o_v[cols, :] = fh[h, 3 * HS :, :]
    for a, ref in enumerate((q_out, k_out, v_out)):
        written.append(fetch(g_v.at[a], ref))
    written.append(fetch(o_v, o_out))
    copy.finish()
    for c in written:
        c.wait()


def hand_over(*refs):
    for src, dst in zip(refs[:5], refs[5:]):
        dst[...] = src[...]


def local(spans, frame_span, norm_gain, w_query, w_key, w_value, w_out, grad_out):
    vmem = pl.BlockSpec(memory_space=pltpu.VMEM)
    smem = pl.BlockSpec(memory_space=pltpu.SMEM)
    anywhere = pl.BlockSpec(memory_space=pl.ANY)
    shape = jax.ShapeDtypeStruct
    scratch = [
        ((2, 256, 512), BF),
        ((256, 512), BF),
        ((8, 2, 256, 512), BF),
        ((8, 2, 256, 512), BF),
        ((3, 128, 256), BF),
        ((256, 128), BF),
        ((2, 128, 512), BF),
        ((2, 2, 2, 2, 2, 128, 512), BF),
        ((8, 8, 256), F32),
        ((8, 256), F32),
        ((256, 128), F32),
        ((2, 256, 384), F32),
        ((2, 256, 128), F32),
        ((4, 2, 2, 128, 128), BF),
        ((4, 2, 2, 8, 16, 128), BF),
        ((2, 256, 256), F32),
        ((2, 256, 256), BF),
        ((4, 2, 2, 8, 16, 128), BF),
        ((4, 2, 2, 128, 128), BF),
        ((2, 256, 384), BF),
        ((512, 512), BF),
        ((2, 8, 256), F32),
        ((8, 256), F32),
        ((8, 256), F32),
        ((8, 8, 256), F32),
        ((8, 2, 256, 512), BF),
        ((8, 256, 512), BF),
        ((2, 8, 128, 512), BF),
        ((2, 8, 128, 512), BF),
        ((2, 2, 2, 2, 2, 384, 128), BF),
        ((2, 2, 2, 2, 2, 128, 128), BF),
        ((2, 6, 2, 128, 128), BF),
        ((2, 2, 2, 128, 128), BF),
        ((2, 2, 2, 128, 128), BF),
        ((2, 6, 64, 128), BF),
        ((2, 2, 64, 128), BF),
        ((2, 4, 6, 192, 128), BF),
        ((2, 4, 2, 192, 128), BF),
        ((2, 4, 384, 128), BF),
        ((2, 6, 192, 128), BF),
        ((2, 2, 192, 128), BF),
        ((2, 512, 128), F32),
        ((512, 128), BF),
        ((512, 128), BF),
        ((2, 512, 128), F32),
        ((2, 256, 512), BF),
        ((3, 128, 256), F32),
        ((256, 128), F32),
        ((RULER, 256), F32),
    ]
    out_shape = (
        shape((1, 2, 256, 512), BF),
        shape((128, 256), F32),
        shape((128, 256), F32),
        shape((128, 256), F32),
        shape((256, 128), F32),
    )
    results = pl.pallas_call(
        kernel,
        out_shape=out_shape,
        in_specs=[anywhere, smem, vmem] + [anywhere] * 5,
        out_specs=(anywhere,) * 5,
        scratch_shapes=[pltpu.VMEM(*each) for each in scratch]
        + [pltpu.SemaphoreType.DMA((n,)) for n in (DEPARTURES, ARRIVALS, 16)],
        compiler_params=pltpu.CompilerParams(
            collective_id=0, has_side_effects=True, vmem_limit_bytes=56 * 1024 * 1024
        ),
    )(spans, frame_span, norm_gain, w_query, w_key, w_value, w_out, grad_out)
    return pl.pallas_call(
        hand_over,
        out_shape=out_shape,
        in_specs=[vmem] * 5,
        out_specs=(vmem,) * 5,
    )(*results)


def solution(mesh):
    placed = (
        P("dp", "tm", None, "mp"),
        P("dp", "tm"),
        P("mp"),
        P(("dp", "tm"), "mp"),
        P(("dp", "tm"), "mp"),
        P(("dp", "tm"), "mp"),
        P("mp", ("dp", "tm")),
        P("dp", "tm", None, "mp"),
    )
    return jax.shard_map(
        local,
        mesh=mesh,
        in_specs=placed,
        out_specs=(
            P("dp", "tm", None, "mp"),
            P(("dp", "tm"), "mp"),
            P(("dp", "tm"), "mp"),
            P(("dp", "tm"), "mp"),
            P("mp", ("dp", "tm")),
        ),
        check_vma=False,
    )
```

time: 108 us -> 102 us (0.944)
  Pallas kernels: 106 us -> 101 us
    pallas_call x1, Pallas kernels: 104 us -> 98.7 us  [local(): pl.pallas_call(kernel, out_shape=out_shape, in_specs=[anywhere, smem, vme...]
where the time goes in v3:
time: 102 us
  Pallas kernels  101 us (99%)
  between operations  1.29 us (1%)
    pallas_call x1, Pallas kernels, local(): pl.pallas_call(kernel, out_shape=out_shape, in_specs=[anywhere, smem, vme...  98.7 us
    pallas_call x1, Pallas kernels, local(): pl.pallas_call(hand_over, out_shape=out_shape, in_specs=[vmem] * 5, out_s...  2.2 us

profile of v3, /device:TPU:1, one launch (start us, length us, event | category | flops | bytes accessed | tf_op | source)
XLA Modules:
  0.0 102.2 jit_solution(2598741637076844642)
XLA Ops:
  1.3 98.7 %shard_map.119 = (bf16[1,2,256,512]{3,2,1,0:T(8,128)(2,1)}, f32[128,256]{1,0:T(8,128)}, f32[128,256]{1,0:T(8,128)}, f32[128,256]{1,0:T(8,128)}, f32[256,128]{1,0:T(8,128)}) custom-call(bf16[1,2,256,512]{3,2,1,0:T(8,128)(2,1)} %spans_ref.1, s32[1,1]{1,0:T(1,128)S(6)} %copy.13.which_ref, bf16[512]{0:T(512)(128)(2,1)} %gain_ref.1, bf16[128,256]{1,0:T(8,128)(2,1)} %wq_ref.1, ...), custom_call_target="tpu_custom_call" | custom-call | tf_op jit(solution)/shard_map/pallas_call | solution.py:886
  100.0 2.2 %shard_map.120 = (bf16[1,2,256,512]{3,2,1,0:T(8,128)(2,1)}, f32[128,256]{1,0:T(8,128)}, f32[128,256]{1,0:T(8,128)}, f32[128,256]{1,0:T(8,128)}, f32[256,128]{1,0:T(8,128)}) custom-call(bf16[1,2,256,512]{3,2,1,0:T(8,128)(2,1)} %get-tuple-element.10.refs_0_, f32[128,256]{1,0:T(8,128)} %get-tuple-element.11.refs_1_, f32[128,256]{1,0:T(8,128)} %get-tuple-element.12.refs_2_, ...), custom_call_target="tpu_custom_call" | custom-call | tf_op jit(solution)/shard_map/pallas_call | solution.py:897

commit v4 on v3

--- a/solution.py
+++ b/solution.py
@@ -12,8 +12,8 @@
 BF = jnp.bfloat16
 F32 = jnp.float32
 MESH = pl.DeviceIdType.MESH
-ARRIVALS = 100
-DEPARTURES = 8
+ARRIVALS = 104
+DEPARTURES = 4
 RULER = 6144
 
 ROWS_COLS = (((1,), (1,)), ((), ()))
@@ -142,10 +142,10 @@
     r1,
     rc,
     tc,
-    rf,
-    fs,
-    fr,
-    fh,
+    re,
+    re_o,
+    oc,
+    oc_o,
     span_v,
     g_v,
     o_v,
@@ -173,6 +173,9 @@
     def device(x_at, y_at):
         return (hi(y_at) * 2 + core, x_at * 2 + lo(y_at), mp)
 
+    def device_of(x_at, y_at, core_at):
+        return (hi(y_at) * 2 + core_at, x_at * 2 + lo(y_at), mp)
+
     def ring8(offset):
         return lax.rem(mp + offset + 8, 8)
 
@@ -195,6 +198,8 @@
     partners = [sibling, far_y]
     partners += [along_z(k) for k in range(1, 8)]
     partners += [along_tm(k) for k in range(1, 8)]
+    partners += [device_of(xs[k], y, other) for k in (1, 3)]
+    partners += [device_of(x, ys[k], other) for k in (1, 3)]
     for partner in partners:
         pl.semaphore_signal(barrier, inc=1, device_id=partner, device_id_type=MESH)
 
@@ -464,12 +469,12 @@
 
     away = [grads_out(0)]
     forward_xn(4, 0, 1)
-    ring_dy.take(5, then=(7,))
     for s in range(2):
         for a in range(3):
             for part in range(2):
                 sb[a, part, s] = aq[s, group(part), a * HS : (a + 1) * HS].astype(BF)
     trips = swap_out(pl.ds(0, 3), both)
+    ring_dy.take(5, then=(7,))
     ring_dy.take(6, then=(8,))
     ring_dy.share(5, 6, half=1)
     forward_dy(1, -1, 1, 3)
@@ -480,8 +485,6 @@
     forward_dy(1, -3, 6, 2)
     ring_dy.take(9)
     ring_dy.hand(dy.at[ring8(4), core, pl.ds(128, 128)], 1)
-    forward_dy(1, 4, 0, 1)
-    away.append(grads_out(1))
     trips.wait()
 
     row_id = lax.broadcasted_iota(jnp.int32, (256, 256), 0)
@@ -518,6 +521,8 @@
         return swap_back(pl.ds(1, 3), one[part])
 
     attend(0)
+    forward_dy(1, 4, 0, 1)
+    away.append(grads_out(1))
     back = [attend_back(0)]
     attend(1)
     att_trips = swap_back(pl.ds(0, 1), both)
@@ -537,9 +542,6 @@
             place[i // 2, i % 2] = value[:, i * HS : (i + 1) * HS]
         return carry
 
-    att_trips.wait()
-    keep_transposed(3)
-    lax.fori_loop(0, 8, out_grad, 0)
 
     offsets = (4, 3, -3, 2, -2, 1, -1, 0)
 
@@ -548,51 +550,57 @@
             for a in range(3):
                 gc[s, group(half), a * HS : (a + 1) * HS] = gb[1 + a, half, s]
 
-    def input_grads(half, first, last):
+    needs = (((0, 2), (1, 4), (3, 6), (5, 7)), ((0, 1), (3, 2), (5, 4), (6, 7)))
+
+    def input_grads(half, order):
         met = copy.batch()
         rows = group(half)
-        for index in range(first, last):
+        for index in needs[half][order]:
             w = weights(ring8(offsets[index]), qkv_cols)
             value = dot_t(gc[:, rows, :].reshape(256, 3 * HS), w).astype(BF)
             ps[index, :, rows, :] = value.reshape(2, 128, 512)
             part = pl.ds(half * 128, 128)
             met(ps.at[index, other, part], sr.at[index, part], sibling)
-        across.append(met)
-
-    across = []
-
-    def total_of(index, half):
-        rows = group(half)
+        across[half, order] = met
+
+    across = {}
+
+    def total_of(index, rows):
         return ps[index, core, rows, :].astype(F32) + sr[index, rows, :].astype(F32)
 
     ways = (((4, 3, 2, 1), (3, 2, 1)), ((3, 2, 1), (4, 3, 2, 1)))
     flying = {}
 
     def hop(half, order):
-        if across and order < 2:
-            across.pop().wait()
-        if order:
-            flying[half].wait()
-        flying[half] = copy.batch()
+        across.pop((half, order)).wait()
         slot = half * 4 + order
-        for d in range(2):
-            way = ways[half][d]
-            if order >= len(way):
-                continue
-            distance = way[order]
-            offset = 4 if distance == 4 else (distance, -distance)[d]
-            value = total_of(offsets.index(offset), half)
+        for quarter in range(2):
             if order:
-                value = value + cr[d, slot - 1].astype(F32)
-            cs[d, slot] = value.astype(BF)
-            flying[half](cs.at[d, slot], cr.at[d, slot], (zr, zl)[d])
+                flying[half, quarter].wait()
+            trip = copy.batch()
+            flying[half, quarter] = trip
+            part = slice(quarter * 64, quarter * 64 + 64)
+            rows = slice(half * 128 + part.start, half * 128 + part.stop)
+            for d in range(2):
+                way = ways[half][d]
+                if order >= len(way):
+                    continue
+                distance = way[order]
+                offset = 4 if distance == 4 else (distance, -distance)[d]
+                value = total_of(offsets.index(offset), rows)
+                if order:
+                    value = value + cr[d, slot - 1, part, :].astype(F32)
+                cs[d, slot, part, :] = value.astype(BF)
+                place = (d, slot, pl.ds(part.start, 64))
+                trip(cs.at[place], cr.at[place], (zr, zl)[d])
 
     class Reduce:
-        def __init__(self, part, right, left, got, tmp):
+        def __init__(self, part, right, left, got, tmp, end=None):
             self.part = part
             self.to = (right, left)
             self.got = got
             self.tmp = tmp
+            self.ends, self.slots, self.second = end or (self.to, got, None)
 
         def far(self):
             self.first = copy.batch()
@@ -600,23 +608,36 @@
             self.first(self.part(2, 1), self.got.at[1], self.to[1])
 
         def near(self):
-            self.second = copy.batch()
-            self.second(self.part(1, 1), self.got.at[2], self.to[0])
-            self.second(self.part(3, 0), self.got.at[3], self.to[1])
+            if self.second is None:
+                self.second = copy.batch()
+            self.second(self.part(1, 1), self.slots.at[2], self.ends[0])
+            self.second(self.part(3, 0), self.slots.at[3], self.ends[1])
 
         def chain(self):
             self.first.wait()
             for d, (at, half) in enumerate(((1, 0), (3, 1))):
                 value = self.part(at, half)[...].astype(F32) + self.got[d].astype(F32)
                 self.tmp[d] = value.astype(BF)
-                self.second(self.tmp.at[d], self.got.at[4 + d], self.to[d])
+                self.second(self.tmp.at[d], self.slots.at[4 + d], self.ends[d])
 
         def finish(self):
-            got = self.got
             self.second.wait()
-            first = self.part(0, 0)[...].astype(F32) + got[3].astype(F32) + got[4].astype(F32)
-            second = self.part(0, 1)[...].astype(F32) + got[2].astype(F32) + got[5].astype(F32)
-            return first, second
+            return joined(self.part(0, 0)[...], self.part(0, 1)[...], self.slots)
+
+    def joined(first, second, got):
+        return (
+            first.astype(F32) + got[3].astype(F32) + got[4].astype(F32),
+            second.astype(F32) + got[2].astype(F32) + got[5].astype(F32),
+        )
+
+    ending = copy.batch()
+
+    def end_of(axis, slots):
+        if axis == 0:
+            ends = device_of(xs[1], y, axis), device_of(xs[3], y, axis)
+        else:
+            ends = device_of(x, ys[1], axis), device_of(x, ys[3], axis)
+        return ends, slots.at[core], ending
 
     def out_first(axis):
         def part_a(j, half):
@@ -635,17 +656,25 @@
             return r1_o.at[axis, hi(ring[j]), lo(ring[j]), pl.ds(half * 64, 64)]
 
         right, left = ((xr, xl), (yr, yd))[axis]
-        return Reduce(part, right, left, rc_o.at[axis], tc_o.at[axis])
+        end = end_of(axis, re_o)
+        return Reduce(part, right, left, rc_o.at[axis], tc_o.at[axis], end)
 
     out1 = [out_first(axis) for axis in range(2)]
     out2 = [out_second(axis) for axis in range(2)]
+    back[0].wait()
+    grads_in(0)
+    input_grads(0, 0)
+    att_trips.wait()
+    keep_transposed(3)
+    lax.fori_loop(0, 8, out_grad, 0)
     for stage in out1:
         stage.far()
         stage.near()
-    back[0].wait()
-    grads_in(0)
-    input_grads(0, 0, 3)
+    hop(0, 0)
+    input_grads(0, 1)
     back[1].wait()
+    grads_in(1)
+    input_grads(1, 0)
 
     for a in range(3):
         keep_transposed(a)
@@ -683,15 +712,11 @@
             return r1.at[axis, j, half_rows(half)]
 
         right, left = ((xr, xl), (yr, yd))[axis]
-        return Reduce(part, right, left, rc.at[axis], tc.at[axis])
+        end = end_of(axis, re)
+        return Reduce(part, right, left, rc.at[axis], tc.at[axis], end)
 
     stage1 = [[first_stage(axis, k) for k in range(4)] for axis in range(2)]
     stage2 = [second_stage(axis) for axis in range(2)]
-
-    def begin(k):
-        for axis in range(2):
-            stage1[axis][k].far()
-            stage1[axis][k].near()
 
     def chain(k):
         for axis in range(2):
@@ -702,44 +727,29 @@
             for half, value in enumerate(stage1[axis][k].finish()):
                 r1[axis, k, half_rows(half), :] = value.astype(BF)
 
+    def start(axis, *groups):
+        for k in groups:
+            stage1[axis][k].far()
+            stage1[axis][k].near()
+
     grads(lambda i: (i, 0, 1 - xh))
-    stage1[0][2].far()
-    stage1[0][2].near()
-    hop(0, 0)
+    start(0, 2)
+    hop(1, 0)
     grads(lambda i: (1 - yh, 1, i))
-    stage1[1][2].far()
-    stage1[1][2].near()
-    grads_in(1)
-    input_grads(1, 0, 3)
+    start(1, 2)
     grads(lambda i: (i, 0, xh))
-    for k in (1, 3):
-        stage1[0][k].far()
-        stage1[0][k].near()
-    hop(1, 0)
+    start(0, 1, 3, 0)
+    hop(0, 1)
     grads(lambda i: (yh, 1, i))
-    for k in (1, 3):
-        stage1[1][k].far()
-        stage1[1][k].near()
-    input_grads(0, 3, 8)
+    start(1, 1, 3, 0)
+    input_grads(1, 1)
     chain(2)
-    hop(0, 1)
-    begin(0)
     for stage in out1:
         stage.chain()
-    input_grads(1, 3, 8)
-    chain(1)
-    chain(3)
+    input_grads(0, 2)
     hop(1, 1)
-    finish(2)
-    for axis in range(2):
-        stage2[axis].far()
     hop(0, 2)
-    for axis in range(2):
-        for half, value in enumerate(out1[axis].finish()):
-            r1_o[axis, half] = value.astype(BF)
-        out2[axis].far()
-        out2[axis].near()
-    chain(0)
+    input_grads(1, 2)
 
     for s in range(2):
         prod = jnp.zeros((256, HS), F32)
@@ -750,32 +760,45 @@
         ts[s] = jnp.broadcast_to(jnp.sum(prod.T, axis=0, keepdims=True), (8, 256))
     inner_pair = copy(ts.at[other], tr, sibling)
 
+    chain(1)
+    chain(3)
+    finish(2)
+    for axis in range(2):
+        stage2[axis].far()
     hop(1, 2)
-    for stage in out2:
-        stage.chain()
-    finish(1)
-    finish(3)
+    input_grads(0, 3)
+    input_grads(1, 3)
+    chain(0)
+    hop(0, 3)
     for axis in range(2):
-        stage2[axis].near()
+        for half, value in enumerate(out1[axis].finish()):
+            r1_o[axis, half] = value.astype(BF)
+        out2[axis].far()
+        out2[axis].near()
     inner_pair.wait()
     tl[...] = ts[core] + tr[...]
     tt[mp] = tl[...]
     inner = copy.batch()
     for k in range(1, 8):
         inner(tl, tt.at[mp], along_z(k))
-    hop(0, 3)
+    finish(1)
+    finish(3)
+    for axis in range(2):
+        stage2[axis].near()
+    hop(1, 3)
+    for stage in out2:
+        stage.chain()
+    finish(0)
     for axis in range(2):
         stage2[axis].chain()
-    hop(1, 3)
-    finish(0)
-    for axis in range(2):
-        for half, value in enumerate(out2[axis].finish()):
-            rf[axis, 384 + half * 64 : 448 + half * 64, :] = value
-        for half, value in enumerate(stage2[axis].finish()):
-            rf[axis, half_rows(half), :] = value
-    fs[...] = rf[other].astype(BF)
-    last = copy(fs, fr, sibling)
-    fh[core] = rf[core]
+
+    def out_place(axis):
+        return r1_o.at[axis, xh + axis * (yh - xh), lo(x) + axis * (yl - lo(x))]
+
+    ending(r1.at[other, 0], oc.at[core], sibling)
+    ending(out_place(other), oc_o.at[core], sibling)
+    oc[core] = r1[core, 0]
+    oc_o[core] = out_place(core)[...]
 
     inner.wait()
     inner_row = tt[0]
@@ -784,8 +807,9 @@
     inner_col = jnp.broadcast_to(inner_row[0:1, :] / 4096.0, (HS, 256)).T
     for half in range(2):
         rows = group(half)
-        flying[half].wait()
-        grad = total_of(7, half)
+        for quarter in range(2):
+            flying[half, quarter].wait()
+        grad = total_of(7, rows)
         for d in range(2):
             final = len(ways[half][d]) - 1
             grad = grad + cr[d, half * 4 + final].astype(F32)
@@ -800,13 +824,16 @@
                 span_v[j, rows, cols] = jnp.where(which == j, value, jnp.zeros_like(value))
     written = [fetch(span_v, span_out.at[0])]
 
-    last.wait()
-    fh[other] = fr[...].astype(F32)
+    ending.wait()
     for h in range(2):
         cols = slice(h * HS, (h + 1) * HS)
+        halves_of = joined(oc[h, :192, :], oc[h, 192:, :], re.at[h])
+        whole = jnp.concatenate(halves_of, axis=0)
         for a in range(3):
-            g_v[a, :, cols] = fh[h, a * HS : (a + 1) * HS, :].T
-        o_v[cols, :] = fh[h, 3 * HS :, :]
+            g_v[a, :, cols] = whole[a * HS : (a + 1) * HS, :].T
+        first, second = joined(oc_o[h, :64, :], oc_o[h, 64:, :], re_o.at[h])
+        o_v[h * HS : h * HS + 64, :] = first
+        o_v[h * HS + 64 : (h + 1) * HS, :] = second
     for a, ref in enumerate((q_out, k_out, v_out)):
         written.append(fetch(g_v.at[a], ref))
     written.append(fetch(o_v, o_out))
@@ -816,8 +843,16 @@
 
 
 def hand_over(*refs):
-    for src, dst in zip(refs[:5], refs[5:]):
-        dst[...] = src[...]
+    ins, outs, held, sems = refs[:5], refs[5:10], refs[10:15], refs[15]
+    fetched = [pltpu.make_async_copy(ins[i], held[i], sems.at[0, i]) for i in range(5)]
+    written = [pltpu.make_async_copy(held[i], outs[i], sems.at[1, i]) for i in range(5)]
+    for c in fetched:
+        c.start()
+    for i in range(5):
+        fetched[i].wait()
+        written[i].start()
+    for c in written:
+        c.wait()
 
 
 def local(spans, frame_span, norm_gain, w_query, w_key, w_value, w_out, grad_out):
@@ -867,10 +902,10 @@
         ((2, 4, 384, 128), BF),
         ((2, 6, 192, 128), BF),
         ((2, 2, 192, 128), BF),
-        ((2, 512, 128), F32),
-        ((512, 128), BF),
-        ((512, 128), BF),
-        ((2, 512, 128), F32),
+        ((2, 6, 192, 128), BF),
+        ((2, 6, 64, 128), BF),
+        ((2, 384, 128), BF),
+        ((2, 128, 128), BF),
         ((2, 256, 512), BF),
         ((3, 128, 256), F32),
         ((256, 128), F32),
@@ -889,7 +924,7 @@
         in_specs=[anywhere, smem, vmem] + [anywhere] * 5,
         out_specs=(anywhere,) * 5,
         scratch_shapes=[pltpu.VMEM(*each) for each in scratch]
-        + [pltpu.SemaphoreType.DMA((n,)) for n in (DEPARTURES, ARRIVALS, 16)],
+        + [pltpu.SemaphoreType.DMA((n,)) for n in (DEPARTURES, ARRIVALS, 11)],
         compiler_params=pltpu.CompilerParams(
             collective_id=0, has_side_effects=True, vmem_limit_bytes=56 * 1024 * 1024
         ),
@@ -897,8 +932,10 @@
     return pl.pallas_call(
         hand_over,
         out_shape=out_shape,
-        in_specs=[vmem] * 5,
-        out_specs=(vmem,) * 5,
+        in_specs=[anywhere] * 5,
+        out_specs=(anywhere,) * 5,
+        scratch_shapes=[pltpu.VMEM(each.shape, each.dtype) for each in out_shape]
+        + [pltpu.SemaphoreType.DMA((2, 5))],
     )(*results)
 
 

time: 102 us -> 101 us (level)
  Pallas kernels: 101 us -> 99.3 us
    pallas_call x1, Pallas kernels: 98.7 us -> 97.2 us  [local(): pl.pallas_call(kernel, out_shape=out_shape, in_specs=[anywhere, smem, vme...]
where the time goes in v4:
time: 101 us
  Pallas kernels  99.3 us (98%)
  between operations  1.29 us (1%)
    pallas_call x1, Pallas kernels, local(): pl.pallas_call(kernel, out_shape=out_shape, in_specs=[anywhere, smem, vme...  97.2 us
    pallas_call x1, Pallas kernels, local(): pl.pallas_call(hand_over, out_shape=out_shape, in_specs=[anywhere] * 5, o...  2.09 us

profile of v4, /device:TPU:1, one launch (start us, length us, event | category | flops | bytes accessed | tf_op | source)
XLA Modules:
  0.0 100.6 jit_solution(15207931805447441702)
XLA Ops:
  1.3 97.2 %shard_map.119 = (bf16[1,2,256,512]{3,2,1,0:T(8,128)(2,1)}, f32[128,256]{1,0:T(8,128)}, f32[128,256]{1,0:T(8,128)}, f32[128,256]{1,0:T(8,128)}, f32[256,128]{1,0:T(8,128)}) custom-call(bf16[1,2,256,512]{3,2,1,0:T(8,128)(2,1)} %spans_ref.1, s32[1,1]{1,0:T(1,128)S(6)} %copy.13.which_ref, bf16[512]{0:T(512)(128)(2,1)} %gain_ref.1, bf16[128,256]{1,0:T(8,128)(2,1)} %wq_ref.1, ...), custom_call_target="tpu_custom_call" | custom-call | tf_op jit(solution)/shard_map/pallas_call | solution.py:921
  98.5 2.1 %shard_map.120 = (bf16[1,2,256,512]{3,2,1,0:T(8,128)(2,1)}, f32[128,256]{1,0:T(8,128)}, f32[128,256]{1,0:T(8,128)}, f32[128,256]{1,0:T(8,128)}, f32[256,128]{1,0:T(8,128)}) custom-call(bf16[1,2,256,512]{3,2,1,0:T(8,128)(2,1)} %get-tuple-element.10.refs_0_, f32[128,256]{1,0:T(8,128)} %get-tuple-element.11.refs_1_, f32[128,256]{1,0:T(8,128)} %get-tuple-element.12.refs_2_, ...), custom_call_target="tpu_custom_call" | custom-call | tf_op jit(solution)/shard_map/pallas_call | solution.py:932

commit v5 on v4

--- a/solution.py
+++ b/solution.py
@@ -521,15 +521,15 @@
         return swap_back(pl.ds(1, 3), one[part])
 
     attend(0)
+    attend(1)
     forward_dy(1, 4, 0, 1)
     away.append(grads_out(1))
+    att_trips = swap_back(pl.ds(0, 1), both)
     back = [attend_back(0)]
-    attend(1)
-    att_trips = swap_back(pl.ds(0, 1), both)
     back.append(attend_back(1))
 
-    def keep_transposed(a):
-        for part in range(2):
+    def keep_transposed(a, parts=(0, 1)):
+        for part in parts:
             for s in range(2):
                 first = s * 256 + part * 128
                 source = gb[(a + 1) % 4, part, s].astype(F32)
@@ -661,15 +661,17 @@
 
     out1 = [out_first(axis) for axis in range(2)]
     out2 = [out_second(axis) for axis in range(2)]
-    back[0].wait()
-    grads_in(0)
-    input_grads(0, 0)
     att_trips.wait()
     keep_transposed(3)
     lax.fori_loop(0, 8, out_grad, 0)
     for stage in out1:
         stage.far()
         stage.near()
+    back[0].wait()
+    grads_in(0)
+    input_grads(0, 0)
+    for a in range(3):
+        keep_transposed(a, (0,))
     hop(0, 0)
     input_grads(0, 1)
     back[1].wait()
@@ -677,7 +679,7 @@
     input_grads(1, 0)
 
     for a in range(3):
-        keep_transposed(a)
+        keep_transposed(a, (1,))
 
     def weight_grad(yh_at, s_at, xh_at):
         m = (yh_at * 2 + s_at) * 2 + xh_at
@@ -732,11 +734,15 @@
             stage1[axis][k].far()
             stage1[axis][k].near()
 
-    grads(lambda i: (i, 0, 1 - xh))
-    start(0, 2)
+    weight_grad(1 - yh, 0, 1 - xh)
+    stage1[0][2].far()
+    weight_grad(yh, 0, 1 - xh)
+    stage1[0][2].near()
     hop(1, 0)
-    grads(lambda i: (1 - yh, 1, i))
-    start(1, 2)
+    weight_grad(1 - yh, 1, 1 - xh)
+    stage1[1][2].far()
+    weight_grad(1 - yh, 1, xh)
+    stage1[1][2].near()
     grads(lambda i: (i, 0, xh))
     start(0, 1, 3, 0)
     hop(0, 1)
@@ -761,11 +767,11 @@
     inner_pair = copy(ts.at[other], tr, sibling)
 
     chain(1)
+    hop(1, 2)
     chain(3)
     finish(2)
     for axis in range(2):
         stage2[axis].far()
-    hop(1, 2)
     input_grads(0, 3)
     input_grads(1, 3)
     chain(0)

time: 101 us -> 100 us (0.990)
  no operation moved by 1% of the time
where the time goes in v5:
time: 100 us; the launch traced here: 99.9 us
  Pallas kernels  98.6 us (99%)
  between operations  1.29 us (1%)
    pallas_call x1, Pallas kernels, local(): pl.pallas_call(kernel, out_shape=out_shape, in_specs=[anywhere, smem, vme...  96.5 us
    pallas_call x1, Pallas kernels, local(): pl.pallas_call(hand_over, out_shape=out_shape, in_specs=[anywhere] * 5, o...  2.09 us

profile of v5, /device:TPU:1, one launch (start us, length us, event | category | flops | bytes accessed | tf_op | source)
XLA Modules:
  0.0 99.9 jit_solution(16569582550022432859)
XLA Ops:
  1.3 96.5 %shard_map.119 = (bf16[1,2,256,512]{3,2,1,0:T(8,128)(2,1)}, f32[128,256]{1,0:T(8,128)}, f32[128,256]{1,0:T(8,128)}, f32[128,256]{1,0:T(8,128)}, f32[256,128]{1,0:T(8,128)}) custom-call(bf16[1,2,256,512]{3,2,1,0:T(8,128)(2,1)} %spans_ref.1, s32[1,1]{1,0:T(1,128)S(6)} %copy.13.which_ref, bf16[512]{0:T(512)(128)(2,1)} %gain_ref.1, bf16[128,256]{1,0:T(8,128)(2,1)} %wq_ref.1, ...), custom_call_target="tpu_custom_call" | custom-call | tf_op jit(solution)/shard_map/pallas_call | solution.py:927
  97.8 2.1 %shard_map.120 = (bf16[1,2,256,512]{3,2,1,0:T(8,128)(2,1)}, f32[128,256]{1,0:T(8,128)}, f32[128,256]{1,0:T(8,128)}, f32[128,256]{1,0:T(8,128)}, f32[256,128]{1,0:T(8,128)}) custom-call(bf16[1,2,256,512]{3,2,1,0:T(8,128)(2,1)} %get-tuple-element.10.refs_0_, f32[128,256]{1,0:T(8,128)} %get-tuple-element.11.refs_1_, f32[128,256]{1,0:T(8,128)} %get-tuple-element.12.refs_2_, ...), custom_call_target="tpu_custom_call" | custom-call | tf_op jit(solution)/shard_map/pallas_call | solution.py:938

commit v6 on v5

--- a/solution.py
+++ b/solution.py
@@ -832,17 +832,17 @@
 
     ending.wait()
     for h in range(2):
-        cols = slice(h * HS, (h + 1) * HS)
-        halves_of = joined(oc[h, :192, :], oc[h, 192:, :], re.at[h])
-        whole = jnp.concatenate(halves_of, axis=0)
-        for a in range(3):
-            g_v[a, :, cols] = whole[a * HS : (a + 1) * HS, :].T
         first, second = joined(oc_o[h, :64, :], oc_o[h, 64:, :], re_o.at[h])
         o_v[h * HS : h * HS + 64, :] = first
         o_v[h * HS + 64 : (h + 1) * HS, :] = second
+    written.append(fetch(o_v, o_out))
+    wholes = [
+        jnp.concatenate(joined(oc[h, :192, :], oc[h, 192:, :], re.at[h]), axis=0) for h in range(2)
+    ]
     for a, ref in enumerate((q_out, k_out, v_out)):
+        for h in range(2):
+            g_v[a, :, h * HS : (h + 1) * HS] = wholes[h][a * HS : (a + 1) * HS, :].T
         written.append(fetch(g_v.at[a], ref))
-    written.append(fetch(o_v, o_out))
     copy.finish()
     for c in written:
         c.wait()

time: 100 us -> 100 us (level)
  no operation moved by 1% of the time
where the time goes in v6:
time: 100 us; the launch traced here: 99.8 us
  Pallas kernels  98.5 us (98%)
  between operations  1.29 us (1%)
    pallas_call x1, Pallas kernels, local(): pl.pallas_call(kernel, out_shape=out_shape, in_specs=[anywhere, smem, vme...  96.4 us
    pallas_call x1, Pallas kernels, local(): pl.pallas_call(hand_over, out_shape=out_shape, in_specs=[anywhere] * 5, o...  2.09 us

profile of v6, /device:TPU:1, one launch (start us, length us, event | category | flops | bytes accessed | tf_op | source)
XLA Modules:
  0.0 99.8 jit_solution(15027402215498509828)
XLA Ops:
  1.3 96.4 %shard_map.119 = (bf16[1,2,256,512]{3,2,1,0:T(8,128)(2,1)}, f32[128,256]{1,0:T(8,128)}, f32[128,256]{1,0:T(8,128)}, f32[128,256]{1,0:T(8,128)}, f32[256,128]{1,0:T(8,128)}) custom-call(bf16[1,2,256,512]{3,2,1,0:T(8,128)(2,1)} %spans_ref.1, s32[1,1]{1,0:T(1,128)S(6)} %copy.13.which_ref, bf16[512]{0:T(512)(128)(2,1)} %gain_ref.1, bf16[128,256]{1,0:T(8,128)(2,1)} %wq_ref.1, ...), custom_call_target="tpu_custom_call" | custom-call | tf_op jit(solution)/shard_map/pallas_call | solution.py:927
  97.7 2.1 %shard_map.120 = (bf16[1,2,256,512]{3,2,1,0:T(8,128)(2,1)}, f32[128,256]{1,0:T(8,128)}, f32[128,256]{1,0:T(8,128)}, f32[128,256]{1,0:T(8,128)}, f32[256,128]{1,0:T(8,128)}) custom-call(bf16[1,2,256,512]{3,2,1,0:T(8,128)(2,1)} %get-tuple-element.10.refs_0_, f32[128,256]{1,0:T(8,128)} %get-tuple-element.11.refs_1_, f32[128,256]{1,0:T(8,128)} %get-tuple-element.12.refs_2_, ...), custom_call_target="tpu_custom_call" | custom-call | tf_op jit(solution)/shard_map/pallas_call | solution.py:938
